TPU v7x, 32 devices: a whole 2x2x4 slice. The times are simulated.
32 devices in a mesh: seq: 16 (over z, y, core), chan: 2 (over x).
Axes of the slice: x: 2, y: 2, z: 4, core: 2. Of those that a mesh axis runs over, the one named last changes fastest.
Arguments:
- tokens: bfloat16 [384, 512, 1024], P('chan', 'seq'), may hold values from -6 to 6
- gating: bfloat16 [384, 512, 1024], P(None, ('seq', 'chan')), may hold values from -6 to 6
- kernel: bfloat16 [384, 1024, 512], P('chan', 'seq'), may hold values from -6 to 6
- first_factor: bfloat16 [1024, 1024], replicated, may hold values from -0.1875 to 0.1875
- first_twiddle: float32 [512, 1024], P('seq'), may hold values from 0.5 to 1.5
- second_factor: bfloat16 [512, 512], replicated, may hold values from -0.25 to 0.25
- inverse_second: bfloat16 [512, 512], replicated, may hold values from -0.25 to 0.25
- inverse_twiddle: float32 [1024, 512], P('seq'), may hold values from 0.5 to 1.5
- inverse_first: bfloat16 [1024, 1024], replicated, may hold values from -0.1875 to 0.1875
- projection: bfloat16 [384, 384], replicated, may hold values from -0.3125 to 0.3125
Outputs:
- result: bfloat16 [384, 512, 1024], P(None, ('seq', 'chan'))
All inputs are finite; a program needn't handle non-finite values.
Results may differ from a plain program's by a relative error of at most 0.012.
Values may be sent and summed in bfloat16 or wider, within the bound.
No kernel may reach another device: no remote copies, remote signals or barrier semaphores. Data moves between devices by JAX's collectives and lax.ppermute only.
A program may use at most 192 MiB of HBM per device.

v0:
```python
import jax
import jax.numpy as jnp
from jax import lax
from jax.sharding import PartitionSpec as P


def body(
    tokens,
    gating,
    kernel,
    first_factor,
    first_twiddle,
    second_factor,
    inverse_second,
    inverse_twiddle,
    inverse_first,
    projection,
):
    seq_count = lax.axis_size("seq")
    chan_count = lax.axis_size("chan")
    channels, local_rows, order_inner = tokens.shape
    order_outer = second_factor.shape[0]
    block_cols = order_inner // seq_count
    chan_rows = local_rows // chan_count
    first_split = first_factor.reshape(seq_count, block_cols, order_inner)
    forward = jnp.einsum("cab,skb->scka", tokens, first_split, preferred_element_type=jnp.float32)
    twiddle = first_twiddle.reshape(local_rows, seq_count, block_cols).transpose(1, 2, 0)
    forward = (forward * twiddle[:, None]).astype(jnp.bfloat16)
    forward = forward.reshape(seq_count, 1, channels, block_cols * local_rows)
    received = lax.all_to_all(forward, "seq", split_axis=0, concat_axis=1, tiled=True)
    received = received.reshape(seq_count, channels, block_cols, local_rows)
    second_split = second_factor.reshape(order_outer, seq_count, local_rows)
    spectrum = jnp.einsum(
        "scka,jsa->ckj", received, second_split, preferred_element_type=jnp.float32
    )
    scaled = (spectrum * kernel).astype(jnp.bfloat16)
    first_join = inverse_first.reshape(order_inner, seq_count, block_cols)
    inverse_split = inverse_second.reshape(seq_count, local_rows, order_outer)
    inverse = jnp.einsum("ckj,sij->scki", scaled, inverse_split, preferred_element_type=jnp.float32)
    twiddle_back = inverse_twiddle.reshape(block_cols, seq_count, local_rows).transpose(1, 0, 2)
    inverse = (inverse * twiddle_back[:, None]).astype(jnp.bfloat16)
    inverse = inverse.reshape(seq_count, 1, channels, block_cols * local_rows)
    returned = lax.all_to_all(inverse, "seq", split_axis=0, concat_axis=1, tiled=True)
    returned = returned.reshape(seq_count, channels, block_cols, local_rows)
    mixed_rows = jnp.einsum(
        "scki,bsk->cib", returned, first_join, preferred_element_type=jnp.float32
    ).astype(jnp.bfloat16)
    mixed_rows = mixed_rows.reshape(channels, chan_count, chan_rows, order_inner)
    mixed_rows = lax.all_to_all(mixed_rows, "chan", split_axis=1, concat_axis=0, tiled=True)
    mixed_rows = mixed_rows.reshape(channels * chan_count, chan_rows, order_inner)
    gated_rows = (mixed_rows.astype(jnp.float32) * gating.astype(jnp.float32)).astype(jnp.bfloat16)
    result_rows = jnp.einsum(
        "cab,ce->eab", gated_rows, projection, preferred_element_type=jnp.float32
    )
    return result_rows.astype(jnp.bfloat16)


def solution(mesh):
    return jax.shard_map(
        body,
        mesh=mesh,
        in_specs=(
            P("chan", "seq", None),
            P(None, ("seq", "chan"), None),
            P("chan", "seq", None),
            P(),
            P("seq", None),
            P(),
            P(),
            P("seq", None),
            P(),
            P(),
        ),
        out_specs=P(None, ("seq", "chan"), None),
        check_vma=False,
    )
```

profile of v0, /device:TPU:12, one launch (start us, length us, event | category | flops | bytes accessed | tf_op | source)
XLA Modules:
  0.0 1052.1 jit_solution(10724656276543907648)
XLA Ops:
  0.0 0.0 copy-start
  0.0 1.2 reshape.50
  1.2 0.1 copy.58
  1.3 0.4 copy-done
  1.7 20.6 %fusion.3 = bf16[16,192,64,32]{1,2,3,0:T(8,128)(2,1)S(1)} fusion(f32[16,64,32]{1,2,0:T(8,128)S(1)} %bitcast.89, bf16[16,64,1024,1]{2,1,3,0:T(8,128)(2,1)S(1)} %bitcast.80, bf16[192,32,1024]{2,1,0:T(8,128)(2,1)} %param.10), kind=kOutput, calls=%fused_computation.8 | convolution fusion | flops 12897484800 | bytes 27394048 | tf_op jit(solution)/shard_map/cab,skb->scka/dot_general | solution.py:26
  22.3 11.2 %copy.31 = bf16[16,192,64,32]{1,3,2,0:T(8,128)(2,1)} copy(bf16[16,192,64,32]{1,2,3,0:T(8,128)(2,1)S(1)} %fusion.3) | data formatting | bytes 25165824 | tf_op jit(solution)/shard_map/convert_element_type | solution.py:28
  33.5 20.7 %copy.32 = bf16[16,1,192,2048]{3,2,1,0:T(8,128)(2,1)} copy(bf16[16,1,192,2048]{2,3,0,1:T(8,128)(2,1)} %bitcast.81) | data formatting | bytes 25165824 | tf_op jit(solution)/shard_map/reshape | solution.py:29
  54.2 0.0 copy-start.4
  54.2 0.0 copy-start.5
  54.2 6.4 all-to-all-start
  60.6 0.0 copy-done.4
  60.6 0.2 copy.34
  60.8 0.0 copy-done.5
  60.8 0.1 copy.36
  60.9 271.7 %all-to-all-done = bf16[16,1,192,2048]{3,2,1,0:T(8,128)(2,1)} async-done(((bf16[16,1,192,2048]{3,2,1,0:T(8,128)(2,1)}), bf16[16,1,192,2048]{3,2,1,0:T(8,128)(2,1)}, u32[]{:S(2)}, u32[]{:S(2)}) %all-to-all-start) | async-done | bytes 12582944 | tf_op jit(solution)/shard_map/all_to_all | solution.py:30
  332.7 20.6 %copy.33 = bf16[16,1,192,2048]{2,3,0,1:T(8,128)(2,1)} copy(bf16[16,1,192,2048]{3,2,1,0:T(8,128)(2,1)} %all-to-all-done) | data formatting | bytes 25165824 | tf_op jit(solution)/shard_map/all_to_all | solution.py:30
  353.2 0.0 copy-start.6
  353.2 41.2 %copy.35 = bf16[16,192,64,32]{2,3,0,1:T(8,128)(2,1)} copy(bf16[16,192,64,32]{1,3,2,0:T(8,128)(2,1)} %bitcast.82) | data formatting | bytes 25165824 | tf_op jit(solution)/shard_map/reshape | solution.py:31
  394.5 0.0 copy-done.6
  394.5 27.7 %fusion = bf16[16,192,64,32]{2,3,0,1:T(8,128)(2,1)} fusion(f32[16,64,32]{1,2,0:T(8,128)S(1)} %bitcast.88, bf16[16,32,512,1]{2,1,0,3:T(8,128)(2,1)S(1)} %bitcast.90, bf16[192,64,512]{2,1,0:T(8,128)(2,1)} %param.12, bf16[16,192,64,32]{2,3,0,1:T(8,128)(2,1)} %copy.35, bf16[512,16,32,1]{0,2,1,3:T(8,128)(2,1)S(1)} %bitcast.87), kind=kOutput, calls=%fused_computation.1 | convolution fusion | flops 12916359168 | bytes 38928384 | tf_op jit(solution)/shard_map/ckj,sij->scki/dot_general | solution.py:39
  422.1 42.9 %copy.37 = bf16[16,192,64,32]{1,3,2,0:T(8,128)(2,1)} copy(bf16[16,192,64,32]{2,3,0,1:T(8,128)(2,1)} %fusion) | data formatting | bytes 25165824 | tf_op jit(solution)/shard_map/convert_element_type | solution.py:41
  465.0 20.7 %copy.38 = bf16[16,1,192,2048]{3,2,1,0:T(8,128)(2,1)} copy(bf16[16,1,192,2048]{2,3,0,1:T(8,128)(2,1)} %bitcast.83) | data formatting | bytes 25165824 | tf_op jit(solution)/shard_map/reshape | solution.py:42
  485.7 0.0 copy-start.2
  485.7 5.2 all-to-all-start.1
  490.9 0.0 copy-done.2
  491.0 2.6 copy.40
  493.5 269.4 %all-to-all-done.1 = bf16[16,1,192,2048]{3,2,1,0:T(8,128)(2,1)} async-done(((bf16[16,1,192,2048]{3,2,1,0:T(8,128)(2,1)}), bf16[16,1,192,2048]{3,2,1,0:T(8,128)(2,1)}, u32[]{:S(2)}, u32[]{:S(2)}) %all-to-all-start.1) | async-done | bytes 12582944 | tf_op jit(solution)/shard_map/all_to_all | solution.py:43
  763.0 20.6 %copy.39 = bf16[16,1,192,2048]{2,3,0,1:T(8,128)(2,1)} copy(bf16[16,1,192,2048]{3,2,1,0:T(8,128)(2,1)} %all-to-all-done.1) | data formatting | bytes 25165824 | tf_op jit(solution)/shard_map/all_to_all | solution.py:43
  783.5 0.0 copy-start.3
  783.5 41.3 %copy.41 = bf16[16,192,64,32]{2,3,0,1:T(8,128)(2,1)} copy(bf16[16,192,64,32]{1,3,2,0:T(8,128)(2,1)} %bitcast.84) | data formatting | bytes 25165824 | tf_op jit(solution)/shard_map/reshape | solution.py:44
  824.9 0.0 copy-done.3
  824.9 17.2 %bitcast_convert_fusion = bf16[192,32,1024]{2,1,0:T(8,128)(2,1)S(1)} fusion(bf16[16,192,64,32]{2,3,0,1:T(8,128)(2,1)} %copy.41, bf16[1024,16,64,1]{0,2,1,3:T(8,128)(2,1)S(1)} %bitcast.86), kind=kOutput, calls=%fused_computation.5 | convolution fusion | flops 12891193344 | bytes 27262976 | tf_op jit(solution)/shard_map/scki,bsk->cib/dot_general | solution.py:45
  842.1 1.7 copy.42
  843.8 143.0 %all_to_all.12 = bf16[192,2,16,1024]{3,2,0,1:T(8,128)(2,1)} all-to-all(bf16[192,2,16,1024]{3,2,0,1:T(8,128)(2,1)S(1)} %copy.42), channel_id=1, replica_groups=mesh['seq'=16,'chan'=2] {'chan'}, dimensions={1} | all-to-all | bytes 25165824 | tf_op jit(solution)/shard_map/all_to_all | solution.py:49
  986.8 7.2 bitcast_convert_fusion.1
  994.1 0.0 copy-start.7
  994.1 12.3 %fusion.1 = bf16[384,16,1024]{2,1,0:T(8,128)(2,1)} fusion(f32[192,2,1,16,1024]{4,3,0,1,2:T(8,128)S(1)} %bitcast_convert_fusion.1, bf16[384,16,1024]{2,1,0:T(8,128)(2,1)} %param.11), kind=kLoop, calls=%fused_computation.4 | loop fusion | flops 18874368 | bytes 50331648 | tf_op jit(solution)/shard_map/convert_element_type | solution.py:51
  1006.3 0.0 copy-done.7
  1006.3 0.0 copy-start.1
  1006.3 29.2 %convert_bitcast_fusion = bf16[384,16,1024]{0,2,1:T(8,128)(2,1)} fusion(bf16[384,16,1024]{2,1,0:T(8,128)(2,1)} %fusion.1, bf16[384,384]{1,0:T(8,128)(2,1)S(1)} %copy-done.7), kind=kOutput, calls=%fused_computation.15 | convolution fusion | flops 4838129664 | bytes 25460736 | tf_op jit(solution)/shard_map/cab,ce->eab/dot_general | solution.py:52
  1035.6 16.6 %copy.44 = bf16[384,16,1024]{2,1,0:T(8,128)(2,1)} copy(bf16[384,16,1024]{0,2,1:T(8,128)(2,1)} %convert_bitcast_fusion) | data formatting | bytes 25165824 | tf_op jit(solution)/shard_map/convert_element_type | solution.py:55
  1052.1 0.0 copy-done.1
Async XLA Ops:
  0.0 1.7 copy-start
  54.2 6.4 copy-start.4
  54.2 6.6 copy-start.5
  54.2 278.5 %all-to-all-start = ((bf16[16,1,192,2048]{3,2,1,0:T(8,128)(2,1)}), bf16[16,1,192,2048]{3,2,1,0:T(8,128)(2,1)}, u32[]{:S(2)}, u32[]{:S(2)}) async-start(bf16[16,1,192,2048]{3,2,1,0:T(8,128)(2,1)} %copy.32), calls=%async_computation | async-start | bytes 25165824 | tf_op jit(solution)/shard_map/all_to_all | solution.py:30
  353.2 41.2 %copy-start.6 = (bf16[512,512]{1,0:T(8,128)(2,1)S(1)}, bf16[512,512]{1,0:T(8,128)(2,1)}, u32[]{:S(2)}) copy-start(bf16[512,512]{1,0:T(8,128)(2,1)} %param.16) | copy-start | bytes 1572868
  485.7 5.2 copy-start.2
  485.7 277.3 %all-to-all-start.1 = ((bf16[16,1,192,2048]{3,2,1,0:T(8,128)(2,1)}), bf16[16,1,192,2048]{3,2,1,0:T(8,128)(2,1)}, u32[]{:S(2)}, u32[]{:S(2)}) async-start(bf16[16,1,192,2048]{3,2,1,0:T(8,128)(2,1)} %copy.38), calls=%async_computation.1 | async-start | bytes 25165824 | tf_op jit(solution)/shard_map/all_to_all | solution.py:43
  783.5 41.3 %copy-start.3 = (bf16[1024,1024]{0,1:T(8,128)(2,1)S(1)}, bf16[1024,1024]{0,1:T(8,128)(2,1)}, u32[]{:S(2)}) copy-start(bf16[1024,1024]{0,1:T(8,128)(2,1)} %copy.40) | copy-start | bytes 6291460
  994.1 12.3 %copy-start.7 = (bf16[384,384]{1,0:T(8,128)(2,1)S(1)}, bf16[384,384]{1,0:T(8,128)(2,1)}, u32[]{:S(2)}) copy-start(bf16[384,384]{1,0:T(8,128)(2,1)} %param.19) | copy-start | bytes 884740
  1006.3 45.8 %copy-start.1 = (bf16[1024,1024]{1,0:T(8,128)(2,1)S(1)}, bf16[1024,1024]{1,0:T(8,128)(2,1)}, u32[]{:S(2)}) copy-start(bf16[1024,1024]{1,0:T(8,128)(2,1)} %param.13) | copy-start | bytes 6291460
where the time goes:
time: 1060 us; the launch traced here: 1050 us
  waiting for transfers between devices  541 us (51%)
  local copies, waits for them, and re-layouts  242 us (23%)
  blocking collectives  143 us (13%)
  matrix products  94.7 us (9%)
  other arithmetic  19.5 us (2%)
  starting transfers between devices  11.6 us (1%)
    all_to_all x1, waiting for transfers between devices, body(): lax.all_to_all(forward, 'seq', split_axis=0, concat_axis=1, tiled=True)  272 us
    all_to_all x1, waiting for transfers between devices, body(): lax.all_to_all(inverse, 'seq', split_axis=0, concat_axis=1, tiled=True)  269 us
    all_to_all x1, blocking collectives, body(): lax.all_to_all(mixed_rows, 'chan', split_axis=1, concat_axis=0, tiled=True)  143 us
    convert_element_type x1, local copies, waits for them, and re-layouts, body(): inverse = (inverse * twiddle_back[:, None]).astype(jnp.bfloat16)  42.9 us
    reshape x1, local copies, waits for them, and re-layouts, body(): returned = returned.reshape(seq_count, channels, block_cols, local_rows)  41.3 us
    reshape x1, local copies, waits for them, and re-layouts, body(): received = received.reshape(seq_count, channels, block_cols, local_rows)  41.2 us
    dot_general x1, matrix products, body(): jnp.einsum('cab,ce->eab', gated_rows, projection, preferred_element_type=...  29.2 us
    dot_general x1, matrix products, body(): jnp.einsum('ckj,sij->scki', scaled, inverse_split, preferred_element_type...  27.7 us
  transfers between devices with their start and end apart: 2, of which 2 were waited for; matrix products, arithmetic and copies ran while one was open for 0% of the time, Pallas kernels for 0%

commit v1 on v0

--- a/solution.py
+++ b/solution.py
@@ -1,10 +1,269 @@
+from functools import partial
+
 import jax
 import jax.numpy as jnp
 from jax import lax
+from jax.experimental import pallas as pl
+from jax.experimental.pallas import tpu as pltpu
 from jax.sharding import PartitionSpec as P
 
-
-def body(
+LANES = 128
+VMEM = 48 * 1024 * 1024
+F32 = jnp.float32
+BF16 = jnp.bfloat16
+
+
+def largest_divisor(number, most):
+    return max(d for d in range(1, min(number, most) + 1) if number % d == 0)
+
+
+def dot_nt(left, right):
+    return lax.dot_general(left, right, (((1,), (1,)), ((), ())), preferred_element_type=F32)
+
+
+def regroup(tiles, width):
+    count = len(tiles)
+    if count == 1:
+        return list(tiles)
+    lane = lax.broadcasted_iota(jnp.int32, tiles[0].shape, tiles[0].ndim - 1)
+    out = []
+    for q in range(count):
+        tile = None
+        for r in range(count):
+            shift = ((r - q) * width) % LANES
+            moved = pltpu.roll(tiles[r], shift, tiles[r].ndim - 1) if shift else tiles[r]
+            tile = moved if tile is None else jnp.where(lane >= r * width, moved, tile)
+        out.append(tile)
+    return out
+
+
+def first_kernel(pack, width, tokens_ref, factor_ref, twiddle_ref, out_ref):
+    channels, rows, order = tokens_ref.shape
+    groups = channels // pack
+    left = tokens_ref[...].reshape(channels * rows, order)
+    step = 2 * LANES
+    for at in range(0, order, step):
+        part = dot_nt(left, factor_ref[at : at + step, :])
+        part = part.reshape(channels, rows, step) * twiddle_ref[:, at : at + step][None]
+        for half in range(step // LANES):
+            tile = part[:, :, half * LANES : (half + 1) * LANES].reshape(groups, pack, rows, LANES)
+            moved = regroup([tile[:, r].reshape(groups * rows, LANES) for r in range(pack)], width)
+            base = (at // LANES + half) * pack
+            for q in range(pack):
+                out_ref[base + q] = moved[q].astype(BF16).reshape(groups, rows, LANES)
+
+
+def middle_kernel(pack, recv_ref, kernel_ref, second_ref, back_ref, twiddle_ref, out_ref):
+    sources, groups, rows, _ = recv_ref.shape
+    dests, _, out_rows, _ = out_ref.shape
+    outer = second_ref.shape[0]
+    width = kernel_ref.shape[1]
+    both = 2 if groups % 2 == 0 else 1
+    for at in range(0, groups, both):
+        cols = [recv_ref[:, at + p].reshape(sources * rows, LANES) for p in range(both)]
+        spectrum = jnp.dot(
+            second_ref[...], jnp.concatenate(cols, axis=1), preferred_element_type=F32
+        )
+        kern = [
+            kernel_ref[(at + p) * pack : (at + p + 1) * pack].reshape(pack * width, outer).astype(F32).T
+            for p in range(both)
+        ]
+        scaled = (spectrum * jnp.concatenate(kern, axis=1)).astype(BF16)
+        inverse = jnp.dot(back_ref[...], scaled, preferred_element_type=F32)
+        for p in range(both):
+            part = inverse[:, p * LANES : (p + 1) * LANES] * twiddle_ref[...]
+            out_ref[:, at + p] = part.astype(BF16).reshape(dests, out_rows, LANES)
+
+
+def last_kernel(pack, width, recv_ref, factor_ref, gating_ref, out_ref, wide_ref):
+    sources, _, groups, rows, _ = recv_ref.shape
+    order = factor_ref.shape[0]
+    for t in range(sources // pack):
+        tiles = [
+            recv_ref[t * pack + r, 0].astype(F32).reshape(groups * rows, LANES) for r in range(pack)
+        ]
+        moved = regroup(tiles, width)
+        for q in range(pack):
+            wide_ref[:, q, :, t * LANES : (t + 1) * LANES] = moved[q].astype(BF16).reshape(groups, rows, LANES)
+    left = wide_ref[...].reshape(groups * pack * rows, order)
+    step = 2 * LANES
+    for at in range(0, order, step):
+        mixed = dot_nt(left, factor_ref[at : at + step, :]).astype(BF16)
+        mixed = mixed.reshape(groups * pack, rows, step).astype(F32)
+        gated = mixed * gating_ref[0, :, :, at : at + step].astype(F32)
+        out_ref[0, :, :, at : at + step] = gated.astype(BF16)
+
+
+def project_kernel(count, *refs):
+    gated_refs, (projection_ref, out_ref, left_ref, right_ref) = refs[:count], refs[count:]
+    parts, channels, rows, step = gated_refs[0].shape
+    total = projection_ref.shape[0]
+    tiles = step // LANES
+    for g, ref in enumerate(gated_refs):
+        for x in range(parts):
+            start = (x * (total // parts) + g * channels) * rows
+            for t in range(tiles):
+                left_ref[t, start : start + channels * rows, :] = (
+                    ref[x, :, :, t * LANES : (t + 1) * LANES].astype(F32).reshape(channels * rows, LANES)
+                )
+    for i in range(rows):
+        right = jnp.concatenate(
+            [left_ref[t, pl.ds(i, total, stride=rows), :].astype(BF16) for t in range(tiles)], axis=1
+        )
+        done = jnp.dot(projection_ref[...], right, preferred_element_type=F32)
+        for t in range(tiles):
+            right_ref[t, pl.ds(i, total, stride=rows), :] = done[:, t * LANES : (t + 1) * LANES]
+    for t in range(tiles):
+        out_ref[:, :, t * LANES : (t + 1) * LANES] = right_ref[t].reshape(total, rows, LANES).astype(BF16)
+
+
+def params(grid):
+    return pltpu.CompilerParams(
+        vmem_limit_bytes=VMEM, dimension_semantics=("arbitrary",) * len(grid)
+    )
+
+
+def first_step(tokens, factor, twiddle, at, count, sources):
+    channels, rows, order = tokens.shape
+    width = order // sources
+    pack = LANES // width
+    per = pack * largest_divisor(count // pack, 16 // pack)
+    grid = (count // per,)
+    return pl.pallas_call(
+        partial(first_kernel, pack, width),
+        grid=grid,
+        in_specs=[
+            pl.BlockSpec((per, rows, order), lambda n: (at // per + n, 0, 0)),
+            pl.BlockSpec(factor.shape, lambda n: (0, 0)),
+            pl.BlockSpec(twiddle.shape, lambda n: (0, 0)),
+        ],
+        out_specs=pl.BlockSpec((sources, per // pack, rows, LANES), lambda n: (0, n, 0, 0)),
+        out_shape=jax.ShapeDtypeStruct((sources, count // pack, rows, LANES), BF16),
+        compiler_params=params(grid),
+        cost_estimate=pl.CostEstimate(
+            flops=2 * count * rows * order * order, bytes_accessed=4 * count * rows * order, transcendentals=0
+        ),
+        name="first_factor",
+    )(tokens, factor, twiddle)
+
+
+def middle_step(received, kernel, second, back, twiddle, at, dests):
+    sources, groups, rows, _ = received.shape
+    channels, width, outer = kernel.shape
+    pack = LANES // width
+    per = largest_divisor(groups, 6)
+    grid = (groups // per,)
+    out_rows = outer // dests
+    return pl.pallas_call(
+        partial(middle_kernel, pack),
+        grid=grid,
+        in_specs=[
+            pl.BlockSpec((sources, per, rows, LANES), lambda n: (0, n, 0, 0)),
+            pl.BlockSpec((per * pack, width, outer), lambda n: (at // (per * pack) + n, 0, 0)),
+            pl.BlockSpec(second.shape, lambda n: (0, 0)),
+            pl.BlockSpec(back.shape, lambda n: (0, 0)),
+            pl.BlockSpec(twiddle.shape, lambda n: (0, 0)),
+        ],
+        out_specs=pl.BlockSpec((dests, per, out_rows, LANES), lambda n: (0, n, 0, 0)),
+        out_shape=jax.ShapeDtypeStruct((dests, groups, out_rows, LANES), BF16),
+        compiler_params=params(grid),
+        cost_estimate=pl.CostEstimate(
+            flops=4 * groups * LANES * outer * outer, bytes_accessed=6 * groups * LANES * outer, transcendentals=0
+        ),
+        name="outer_factors",
+    )(received, kernel, second, back, twiddle)
+
+
+def last_step(returned, factor, gating, at, sources):
+    _, parts, groups, rows, _ = returned.shape
+    order = factor.shape[0]
+    width = order // sources
+    pack = LANES // width
+    per = largest_divisor(groups, 32 // pack)
+    grid = (parts, groups // per)
+    return pl.pallas_call(
+        partial(last_kernel, pack, width),
+        grid=grid,
+        in_specs=[
+            pl.BlockSpec((sources, 1, per, rows, LANES), lambda x, n: (0, x, n, 0, 0)),
+            pl.BlockSpec(factor.shape, lambda x, n: (0, 0)),
+            pl.BlockSpec((1, per * pack, rows, order), lambda x, n: (x, at // (per * pack) + n, 0, 0)),
+        ],
+        out_specs=pl.BlockSpec((1, per * pack, rows, order), lambda x, n: (x, n, 0, 0)),
+        out_shape=jax.ShapeDtypeStruct((parts, groups * pack, rows, order), BF16),
+        scratch_shapes=[pltpu.VMEM((per, pack, rows, order), BF16)],
+        compiler_params=params(grid),
+        cost_estimate=pl.CostEstimate(
+            flops=2 * parts * groups * pack * rows * order * order,
+            bytes_accessed=6 * parts * groups * pack * rows * order,
+            transcendentals=0,
+        ),
+        name="last_factor",
+    )(returned, factor, gating)
+
+
+def project_step(gated, projection):
+    parts, channels, rows, order = gated[0].shape
+    total = projection.shape[0]
+    step = 2 * LANES
+    grid = (order // step,)
+    return pl.pallas_call(
+        partial(project_kernel, len(gated)),
+        grid=grid,
+        in_specs=[pl.BlockSpec((parts, channels, rows, step), lambda n: (0, 0, 0, n)) for _ in gated]
+        + [pl.BlockSpec(projection.shape, lambda n: (0, 0))],
+        out_specs=pl.BlockSpec((total, rows, step), lambda n: (0, 0, n)),
+        out_shape=jax.ShapeDtypeStruct((total, rows, order), BF16),
+        scratch_shapes=[pltpu.VMEM((step // LANES, total * rows, LANES), F32)] * 2,
+        compiler_params=params(grid),
+        cost_estimate=pl.CostEstimate(
+            flops=2 * total * total * rows * order, bytes_accessed=4 * total * rows * order, transcendentals=0
+        ),
+        name="projection",
+    )(*gated, projection)
+
+
+def chunked(
+    tokens,
+    gating,
+    kernel,
+    first_factor,
+    first_twiddle,
+    second_factor,
+    inverse_second,
+    inverse_twiddle,
+    inverse_first,
+    projection,
+):
+    sources, parts = lax.axis_size("seq"), lax.axis_size("chan")
+    dests = sources * parts
+    channels, _, order = tokens.shape
+    width = order // sources
+    pack = LANES // width
+    total, out_rows, _ = gating.shape
+    gating = gating.reshape(parts, channels, out_rows, order)
+    twiddle_back = jnp.tile(inverse_twiddle.T, (1, pack))
+    projection = projection.T
+    chunks = 4
+    count = channels // chunks
+    received = []
+    for g in range(chunks):
+        sent = first_step(tokens, first_factor, first_twiddle, g * count, count, sources)
+        received.append(lax.all_to_all(sent, "seq", split_axis=0, concat_axis=0, tiled=True))
+    returned = []
+    for g in range(chunks):
+        sent = middle_step(
+            received[g], kernel, second_factor, inverse_second, twiddle_back, g * count, dests
+        )
+        returned.append(lax.all_to_all(sent, ("seq", "chan"), split_axis=0, concat_axis=0, tiled=True))
+    gated = []
+    for g in range(chunks):
+        back = returned[g].reshape(sources, parts, count // pack, out_rows, LANES)
+        gated.append(last_step(back, inverse_first, gating, g * count, sources))
+    return project_step(gated, projection)
+
+
+def plain(
     tokens,
     gating,
     kernel,
@@ -55,6 +314,13 @@
     return result_rows.astype(jnp.bfloat16)
 
 
+def body(*arrays):
+    tokens, gating = arrays[:2]
+    width = tokens.shape[2] // lax.axis_size("seq")
+    whole_tiles = gating.shape[1] % 16 == 0 and tokens.shape[1] % 16 == 0 and LANES % width == 0
+    return chunked(*arrays) if whole_tiles else plain(*arrays)
+
+
 def solution(mesh):
     return jax.shard_map(
         body,

time: 1060 us -> 648 us (0.61)
  local copies, waits for them, and re-layouts: 242 us -> 18 us
  blocking collectives: 143 us -> 0 us
  Pallas kernels: 0 us -> 102 us
  matrix products: 94.7 us -> 0 us
  waiting for transfers between devices: 541 us -> 475 us
  starting transfers between devices: 11.6 us -> 47.2 us
  other arithmetic: 19.5 us -> 0 us
    all_to_all x1 -> x0, blocking collectives: 143 us -> none  [body(): lax.all_to_all(mixed_rows, 'chan', split_axis=1, concat_axis=0, tiled=True)]
    reshape x7 -> x0, local copies, waits for them, and re-layouts: 127 us -> none  [the longest x1 41.3 us: body(): returned = returned.reshape(seq_count, channels, block_cols, local_rows)]
    pallas_call x0 -> x13, Pallas kernels: none -> 102 us  [the longest x4 30.8 us: middle_step(): pl.pallas_call(partial(middle_kernel, pack), grid=grid, in_specs=[pl.Bloc...]
    dot_general x4 -> x0, matrix products: 94.7 us -> none  [the longest x1 29.2 us: body(): jnp.einsum('cab,ce->eab', gated_rows, projection, preferred_element_type=...]
    convert_element_type x3 -> x0, local copies, waits for them, and re-layouts: 70.7 us -> none  [the longest x1 42.9 us: body(): inverse = (inverse * twiddle_back[:, None]).astype(jnp.bfloat16)]
    all_to_all x2 -> x8, waiting for transfers between devices: 541 us -> 475 us  [the longest x4 249 us: chunked(): lax.all_to_all(sent, 'seq', split_axis=0, concat_axis=0, tiled=True)]
    all_to_all x2 -> x0, local copies, waits for them, and re-layouts: 41.1 us -> none  [the longest x1 20.6 us: body(): lax.all_to_all(forward, 'seq', split_axis=0, concat_axis=1, tiled=True)]
    all_to_all x2 -> x8, starting transfers between devices: 11.6 us -> 47.2 us  [the longest x4 25.6 us: chunked(): lax.all_to_all(sent, ('seq', 'chan'), split_axis=0, concat_axis=0, tiled=...]
  transfers between devices with their start and end apart: 2 -> 8, of which waited for: 2 -> 8; matrix products, arithmetic and copies ran while one was open for 0% -> 0% of each run, Pallas kernels for 0% -> 10%
where the time goes in v1:
time: 648 us; the launch traced here: 642 us
  waiting for transfers between devices  475 us (73%)
  Pallas kernels  102 us (16%)
  starting transfers between devices  47.2 us (7%)
  local copies, waits for them, and re-layouts  18 us (3%)
    all_to_all x4, waiting for transfers between devices, chunked(): lax.all_to_all(sent, 'seq', split_axis=0, concat_axis=0, tiled=True)  249 us
    all_to_all x4, waiting for transfers between devices, chunked(): lax.all_to_all(sent, ('seq', 'chan'), split_axis=0, concat_axis=0, tiled=...  226 us
    pallas_call x4, Pallas kernels, middle_step(): pl.pallas_call(partial(middle_kernel, pack), grid=grid, in_specs=[pl.Bloc...  30.8 us
    all_to_all x4, starting transfers between devices, chunked(): lax.all_to_all(sent, ('seq', 'chan'), split_axis=0, concat_axis=0, tiled=...  25.6 us
    pallas_call x4, Pallas kernels, last_step(): pl.pallas_call(partial(last_kernel, pack, width), grid=grid, in_specs=[pl...  24.6 us
    pallas_call x1, Pallas kernels, project_step(): pl.pallas_call(partial(project_kernel, len(gated)), grid=grid, in_specs=[...  24.2 us
    pallas_call x4, Pallas kernels, first_step(): pl.pallas_call(partial(first_kernel, pack, width), grid=grid, in_specs=[p...  22.2 us
    all_to_all x4, starting transfers between devices, chunked(): lax.all_to_all(sent, 'seq', split_axis=0, concat_axis=0, tiled=True)  21.5 us
  transfers between devices with their start and end apart: 8, of which 8 were waited for; matrix products, arithmetic and copies ran while one was open for 0% of the time, Pallas kernels for 10%

profile of v1, /device:TPU:12, one launch (start us, length us, event | category | flops | bytes accessed | tf_op | source)
XLA Modules:
  0.0 642.2 jit_solution(10981094635825356148)
XLA Ops:
  0.0 1.6 copy-done
  1.6 0.9 copy-done.15
  2.5 5.6 first_factor.5
  8.1 0.0 copy-start.12
  8.1 1.7 copy-done.12
  9.8 6.4 all-to-all-start.2
  16.1 5.6 first_factor.4
  21.7 0.0 copy-start.10
  21.7 1.7 copy-done.10
  23.4 62.6 %all-to-all-done.2.recv_ref = bf16[16,24,32,128]{3,2,1,0:T(8,128)(2,1)} async-done(((bf16[16,24,32,128]{3,2,1,0:T(8,128)(2,1)}), bf16[16,24,32,128]{3,2,1,0:T(8,128)(2,1)}, u32[]{:S(2)}, u32[]{:S(2)}) %all-to-all-start.2) | async-done | bytes 3145760 | tf_op jit(solution)/shard_map/all_to_all | solution.py:252
  86.0 5.1 all-to-all-start
  91.0 5.6 first_factor.7
  96.6 0.0 copy-start.11
  96.6 1.7 copy-done.11
  98.3 62.5 %all-to-all-done.recv_ref = bf16[16,24,32,128]{3,2,1,0:T(8,128)(2,1)} async-done(((bf16[16,24,32,128]{3,2,1,0:T(8,128)(2,1)}), bf16[16,24,32,128]{3,2,1,0:T(8,128)(2,1)}, u32[]{:S(2)}, u32[]{:S(2)}) %all-to-all-start) | async-done | bytes 3145760 | tf_op jit(solution)/shard_map/all_to_all | solution.py:252
  160.9 5.1 all-to-all-start.6
  165.9 5.6 first_factor.6
  171.5 0.0 copy-start.9
  171.5 1.7 copy-done.9
  173.2 62.6 %all-to-all-done.6.recv_ref = bf16[16,24,32,128]{3,2,1,0:T(8,128)(2,1)} async-done(((bf16[16,24,32,128]{3,2,1,0:T(8,128)(2,1)}), bf16[16,24,32,128]{3,2,1,0:T(8,128)(2,1)}, u32[]{:S(2)}, u32[]{:S(2)}) %all-to-all-start.6) | async-done | bytes 3145760 | tf_op jit(solution)/shard_map/all_to_all | solution.py:252
  235.8 5.1 all-to-all-start.4
  240.8 0.0 copy-done.18
  240.9 0.1 copy.13.twiddle_ref
  241.0 8.0 %outer_factors.5 = bf16[32,24,16,128]{3,2,1,0:T(8,128)(2,1)} custom-call(bf16[16,24,32,128]{3,2,1,0:T(8,128)(2,1)} %all-to-all-done.2.recv_ref, bf16[192,64,512]{2,1,0:T(8,128)(2,1)} %kernel_ref.7, bf16[512,512]{1,0:T(8,128)(2,1)S(1)} %copy-done.13, bf16[512,512]{1,0:T(8,128)(2,1)S(1)} %copy-done.14, f32[512,128]{1,0:T(8,128)S(1)} %copy.13.twiddle_ref), custom_call_target="tpu_custom_call" | custom-call | flops 3221225472 | bytes 9437184 | tf_op jit(solution)/shard_map/outer_factors/pallas_call | solution.py:157
  249.0 61.6 %all-to-all-done.4.recv_ref = bf16[16,24,32,128]{3,2,1,0:T(8,128)(2,1)} async-done(((bf16[16,24,32,128]{3,2,1,0:T(8,128)(2,1)}), bf16[16,24,32,128]{3,2,1,0:T(8,128)(2,1)}, u32[]{:S(2)}, u32[]{:S(2)}) %all-to-all-start.4) | async-done | bytes 3145760 | tf_op jit(solution)/shard_map/all_to_all | solution.py:252
  310.7 4.9 all-to-all-start.3
  315.6 7.9 %outer_factors.4 = bf16[32,24,16,128]{3,2,1,0:T(8,128)(2,1)} custom-call(bf16[16,24,32,128]{3,2,1,0:T(8,128)(2,1)} %all-to-all-done.recv_ref, bf16[192,64,512]{2,1,0:T(8,128)(2,1)} %kernel_ref.7, bf16[512,512]{1,0:T(8,128)(2,1)S(1)} %copy-done.13, bf16[512,512]{1,0:T(8,128)(2,1)S(1)} %copy-done.14, f32[512,128]{1,0:T(8,128)S(1)} %copy.13.twiddle_ref), custom_call_target="tpu_custom_call" | custom-call | flops 3221225472 | bytes 9437184 | tf_op jit(solution)/shard_map/outer_factors/pallas_call | solution.py:157
  323.5 60.5 %all-to-all-done.3 = bf16[32,24,16,128]{3,2,1,0:T(8,128)(2,1)} async-done(((bf16[32,24,16,128]{3,2,1,0:T(8,128)(2,1)}), bf16[32,24,16,128]{3,2,1,0:T(8,128)(2,1)}, u32[]{:S(2)}, u32[]{:S(2)}) %all-to-all-start.3) | async-done | bytes 3145760 | tf_op jit(solution)/shard_map/all_to_all | solution.py:258
  384.0 6.9 %all-to-all-start.1 = ((bf16[32,24,16,128]{3,2,1,0:T(8,128)(2,1)}), bf16[32,24,16,128]{3,2,1,0:T(8,128)(2,1)}, u32[]{:S(2)}, u32[]{:S(2)}) async-start(bf16[32,24,16,128]{3,2,1,0:T(8,128)(2,1)} %outer_factors.4), calls=%async_computation.1 | async-start | bytes 6291456 | tf_op jit(solution)/shard_map/all_to_all | solution.py:258
  390.9 8.0 %outer_factors.7 = bf16[32,24,16,128]{3,2,1,0:T(8,128)(2,1)} custom-call(bf16[16,24,32,128]{3,2,1,0:T(8,128)(2,1)} %all-to-all-done.6.recv_ref, bf16[192,64,512]{2,1,0:T(8,128)(2,1)} %kernel_ref.7, bf16[512,512]{1,0:T(8,128)(2,1)S(1)} %copy-done.13, bf16[512,512]{1,0:T(8,128)(2,1)S(1)} %copy-done.14, f32[512,128]{1,0:T(8,128)S(1)} %copy.13.twiddle_ref), custom_call_target="tpu_custom_call" | custom-call | flops 3221225472 | bytes 9437184 | tf_op jit(solution)/shard_map/outer_factors/pallas_call | solution.py:157
  398.9 60.4 %all-to-all-done.1 = bf16[32,24,16,128]{3,2,1,0:T(8,128)(2,1)} async-done(((bf16[32,24,16,128]{3,2,1,0:T(8,128)(2,1)}), bf16[32,24,16,128]{3,2,1,0:T(8,128)(2,1)}, u32[]{:S(2)}, u32[]{:S(2)}) %all-to-all-start.1) | async-done | bytes 3145760 | tf_op jit(solution)/shard_map/all_to_all | solution.py:258
  459.3 6.9 %all-to-all-start.7 = ((bf16[32,24,16,128]{3,2,1,0:T(8,128)(2,1)}), bf16[32,24,16,128]{3,2,1,0:T(8,128)(2,1)}, u32[]{:S(2)}, u32[]{:S(2)}) async-start(bf16[32,24,16,128]{3,2,1,0:T(8,128)(2,1)} %outer_factors.7), calls=%async_computation.7 | async-start | bytes 6291456 | tf_op jit(solution)/shard_map/all_to_all | solution.py:258
  466.2 6.8 %outer_factors.6 = bf16[32,24,16,128]{3,2,1,0:T(8,128)(2,1)S(1)} custom-call(bf16[16,24,32,128]{3,2,1,0:T(8,128)(2,1)} %all-to-all-done.4.recv_ref, bf16[192,64,512]{2,1,0:T(8,128)(2,1)} %kernel_ref.7, bf16[512,512]{1,0:T(8,128)(2,1)S(1)} %copy-done.13, bf16[512,512]{1,0:T(8,128)(2,1)S(1)} %copy-done.14, f32[512,128]{1,0:T(8,128)S(1)} %copy.13.twiddle_ref), custom_call_target="tpu_custom_call" | custom-call | flops 3221225472 | bytes 9437184 | tf_op jit(solution)/shard_map/outer_factors/pallas_call | solution.py:157
  473.1 1.7 copy-done.8
  474.8 59.9 %all-to-all-done.7 = bf16[32,24,16,128]{3,2,1,0:T(8,128)(2,1)} async-done(((bf16[32,24,16,128]{3,2,1,0:T(8,128)(2,1)}), bf16[32,24,16,128]{3,2,1,0:T(8,128)(2,1)}, u32[]{:S(2)}, u32[]{:S(2)}) %all-to-all-start.7) | async-done | bytes 3145760 | tf_op jit(solution)/shard_map/all_to_all | solution.py:258
  534.7 6.9 %all-to-all-start.5 = ((bf16[32,24,16,128]{3,2,1,0:T(8,128)(2,1)}), bf16[32,24,16,128]{3,2,1,0:T(8,128)(2,1)}, u32[]{:S(2)}, u32[]{:S(2)}) async-start(bf16[32,24,16,128]{3,2,1,0:T(8,128)(2,1)} %copy-done.8), calls=%async_computation.5 | async-start | bytes 6291456 | tf_op jit(solution)/shard_map/all_to_all | solution.py:258
  541.6 0.2 copy.17
  541.8 6.1 last_factor.5.refs_1_
  548.0 1.6 copy-done.3
  549.6 6.1 last_factor.4.refs_0_
  555.7 0.0 copy-start.4
  555.7 1.7 copy-done.4
  557.4 6.1 last_factor.7.refs_3_
  563.5 1.7 copy-done.6
  565.2 44.8 %all-to-all-done.5 = bf16[32,24,16,128]{3,2,1,0:T(8,128)(2,1)} async-done(((bf16[32,24,16,128]{3,2,1,0:T(8,128)(2,1)}), bf16[32,24,16,128]{3,2,1,0:T(8,128)(2,1)}, u32[]{:S(2)}, u32[]{:S(2)}) %all-to-all-start.5) | async-done | bytes 3145760 | tf_op jit(solution)/shard_map/all_to_all | solution.py:258
  610.0 6.3 last_factor.6.refs_2_
  616.3 1.7 copy-done.7
  618.0 24.2 %projection.1 = bf16[384,16,1024]{2,1,0:T(8,128)(2,1)} custom-call(bf16[2,48,16,1024]{3,2,1,0:T(8,128)(2,1)S(1)} %copy-done.5, bf16[2,48,16,1024]{3,2,1,0:T(8,128)(2,1)} %copy-done.3, bf16[2,48,16,1024]{3,2,1,0:T(8,128)(2,1)} %copy-done.7, bf16[2,48,16,1024]{3,2,1,0:T(8,128)(2,1)} %copy-done.6, bf16[384,384]{1,0:T(8,128)(2,1)S(1)} %bitcast.8), custom_call_target="tpu_custom_call" | custom-call | flops 4831838208 | bytes 25165824 | tf_op jit(solution)/shard_map/projection/pallas_call | solution.py:210
  (22 shorter events, 0.1 us)
Async XLA Ops:
  0.0 1.6 copy-start
  1.6 0.9 copy-start.15
  8.1 1.7 copy-start.12
  9.8 6.4 copy-start.1
  9.8 6.4 copy-start.16
  9.8 76.2 %all-to-all-start.2 = ((bf16[16,24,32,128]{3,2,1,0:T(8,128)(2,1)}), bf16[16,24,32,128]{3,2,1,0:T(8,128)(2,1)}, u32[]{:S(2)}, u32[]{:S(2)}) async-start(bf16[16,24,32,128]{3,2,1,0:T(8,128)(2,1)} %copy-done.12), calls=%async_computation.2 | async-start | bytes 6291456 | tf_op jit(solution)/shard_map/all_to_all | solution.py:252
  21.7 1.7 copy-start.10
  86.0 74.9 %all-to-all-start = ((bf16[16,24,32,128]{3,2,1,0:T(8,128)(2,1)}), bf16[16,24,32,128]{3,2,1,0:T(8,128)(2,1)}, u32[]{:S(2)}, u32[]{:S(2)}) async-start(bf16[16,24,32,128]{3,2,1,0:T(8,128)(2,1)} %copy-done.10), calls=%async_computation | async-start | bytes 6291456 | tf_op jit(solution)/shard_map/all_to_all | solution.py:252
  96.6 1.7 copy-start.11
  160.9 74.9 %all-to-all-start.6 = ((bf16[16,24,32,128]{3,2,1,0:T(8,128)(2,1)}), bf16[16,24,32,128]{3,2,1,0:T(8,128)(2,1)}, u32[]{:S(2)}, u32[]{:S(2)}) async-start(bf16[16,24,32,128]{3,2,1,0:T(8,128)(2,1)} %copy-done.11), calls=%async_computation.6 | async-start | bytes 6291456 | tf_op jit(solution)/shard_map/all_to_all | solution.py:252
  171.5 1.7 copy-start.9
  173.2 67.7 %copy-start.18 = (f32[64,512]{1,0:T(8,128)S(1)}, f32[64,512]{1,0:T(8,128)}, u32[]{:S(2)}) copy-start(f32[64,512]{1,0:T(8,128)} %param.17) | copy-start | bytes 393220
  173.2 67.8 %copy-start.13 = (bf16[512,512]{1,0:T(8,128)(2,1)S(1)}, bf16[512,512]{1,0:T(8,128)(2,1)}, u32[]{:S(2)}) copy-start(bf16[512,512]{1,0:T(8,128)(2,1)} %second_ref.7) | copy-start | bytes 1572868
  173.2 67.8 %copy-start.14 = (bf16[512,512]{1,0:T(8,128)(2,1)S(1)}, bf16[512,512]{1,0:T(8,128)(2,1)}, u32[]{:S(2)}) copy-start(bf16[512,512]{1,0:T(8,128)(2,1)} %back_ref.7) | copy-start | bytes 1572868
  235.8 74.9 %all-to-all-start.4 = ((bf16[16,24,32,128]{3,2,1,0:T(8,128)(2,1)}), bf16[16,24,32,128]{3,2,1,0:T(8,128)(2,1)}, u32[]{:S(2)}, u32[]{:S(2)}) async-start(bf16[16,24,32,128]{3,2,1,0:T(8,128)(2,1)} %copy-done.9), calls=%async_computation.4 | async-start | bytes 6291456 | tf_op jit(solution)/shard_map/all_to_all | solution.py:252
  310.7 73.3 %all-to-all-start.3 = ((bf16[32,24,16,128]{3,2,1,0:T(8,128)(2,1)}), bf16[32,24,16,128]{3,2,1,0:T(8,128)(2,1)}, u32[]{:S(2)}, u32[]{:S(2)}) async-start(bf16[32,24,16,128]{3,2,1,0:T(8,128)(2,1)} %outer_factors.5), calls=%async_computation.3 | async-start | bytes 6291456 | tf_op jit(solution)/shard_map/all_to_all | solution.py:258
  384.0 75.3 %all-to-all-start.1 = ((bf16[32,24,16,128]{3,2,1,0:T(8,128)(2,1)}), bf16[32,24,16,128]{3,2,1,0:T(8,128)(2,1)}, u32[]{:S(2)}, u32[]{:S(2)}) async-start(bf16[32,24,16,128]{3,2,1,0:T(8,128)(2,1)} %outer_factors.4), calls=%async_computation.1 | async-start | bytes 6291456 | tf_op jit(solution)/shard_map/all_to_all | solution.py:258
  459.3 75.3 %all-to-all-start.7 = ((bf16[32,24,16,128]{3,2,1,0:T(8,128)(2,1)}), bf16[32,24,16,128]{3,2,1,0:T(8,128)(2,1)}, u32[]{:S(2)}, u32[]{:S(2)}) async-start(bf16[32,24,16,128]{3,2,1,0:T(8,128)(2,1)} %outer_factors.7), calls=%async_computation.7 | async-start | bytes 6291456 | tf_op jit(solution)/shard_map/all_to_all | solution.py:258
  473.1 1.7 copy-start.8
  474.8 66.8 %copy-start.17 = (bf16[384,384]{1,0:T(8,128)(2,1)S(1)}, bf16[384,384]{1,0:T(8,128)(2,1)}, u32[]{:S(2)}) copy-start(bf16[384,384]{1,0:T(8,128)(2,1)} %param.19) | copy-start | bytes 884740
  474.8 67.0 %copy-start.2 = (bf16[1024,1024]{1,0:T(8,128)(2,1)S(1)}, bf16[1024,1024]{1,0:T(8,128)(2,1)}, u32[]{:S(2)}) copy-start(bf16[1024,1024]{1,0:T(8,128)(2,1)} %factor_ref.15) | copy-start | bytes 6291460
  534.7 75.3 %all-to-all-start.5 = ((bf16[32,24,16,128]{3,2,1,0:T(8,128)(2,1)}), bf16[32,24,16,128]{3,2,1,0:T(8,128)(2,1)}, u32[]{:S(2)}, u32[]{:S(2)}) async-start(bf16[32,24,16,128]{3,2,1,0:T(8,128)(2,1)} %copy-done.8), calls=%async_computation.5 | async-start | bytes 6291456 | tf_op jit(solution)/shard_map/all_to_all | solution.py:258
  548.0 1.6 copy-start.3
  555.7 1.7 copy-start.4
  563.5 1.7 copy-start.6
  610.0 8.0 %copy-start.5 = (bf16[2,48,16,1024]{3,2,1,0:T(8,128)(2,1)S(1)}, bf16[2,48,16,1024]{3,2,1,0:T(8,128)(2,1)}, u32[]{:S(2)}) copy-start(bf16[2,48,16,1024]{3,2,1,0:T(8,128)(2,1)} %copy-done.4) | copy-start | bytes 9437188
  616.3 1.7 copy-start.7

commit v2 on v1

--- a/solution.py
+++ b/solution.py
@@ -8,7 +8,10 @@
 from jax.sharding import PartitionSpec as P
 
 LANES = 128
-VMEM = 48 * 1024 * 1024
+SUBLANES = 8
+GROUPS = 16
+FIRST = 16
+MIB = 1024 * 1024
 F32 = jnp.float32
 BF16 = jnp.bfloat16
 
@@ -53,73 +56,97 @@
                 out_ref[base + q] = moved[q].astype(BF16).reshape(groups, rows, LANES)
 
 
-def middle_kernel(pack, recv_ref, kernel_ref, second_ref, back_ref, twiddle_ref, out_ref):
-    sources, groups, rows, _ = recv_ref.shape
-    dests, _, out_rows, _ = out_ref.shape
-    outer = second_ref.shape[0]
+def middle_kernel(pack, recv_ref, kernel_ref, second_ref, back_ref, twiddle_ref, out_ref, turn_ref):
+    size = second_ref.shape[0]
+    groups = recv_ref.shape[1]
     width = kernel_ref.shape[1]
     both = 2 if groups % 2 == 0 else 1
     for at in range(0, groups, both):
-        cols = [recv_ref[:, at + p].reshape(sources * rows, LANES) for p in range(both)]
+        cols = [recv_ref[:, at + p].reshape(size, LANES) for p in range(both)]
         spectrum = jnp.dot(
             second_ref[...], jnp.concatenate(cols, axis=1), preferred_element_type=F32
         )
         kern = [
-            kernel_ref[(at + p) * pack : (at + p + 1) * pack].reshape(pack * width, outer).astype(F32).T
+            kernel_ref[(at + p) * pack : (at + p + 1) * pack].reshape(pack * width, size).astype(F32).T
             for p in range(both)
         ]
         scaled = (spectrum * jnp.concatenate(kern, axis=1)).astype(BF16)
         inverse = jnp.dot(back_ref[...], scaled, preferred_element_type=F32)
         for p in range(both):
             part = inverse[:, p * LANES : (p + 1) * LANES] * twiddle_ref[...]
-            out_ref[:, at + p] = part.astype(BF16).reshape(dests, out_rows, LANES)
+            turn_ref[pl.ds(at + p, size, stride=groups), :] = part
+    out_ref[...] = turn_ref[...].astype(BF16).reshape(out_ref.shape)
+
+
+def turn_kernel(pack, gating_ref, out_ref, turn_ref):
+    channels, rows, order = gating_ref.shape
+    groups = channels // pack
+    for t in range(order // LANES):
+        lanes = slice(t * LANES, (t + 1) * LANES)
+        turn_ref[t] = gating_ref[:, :, lanes].astype(F32).reshape(channels * rows, LANES)
+        for r in range(pack):
+            for i in range(rows):
+                part = turn_ref[t, pl.ds(r * rows + i, groups, stride=pack * rows), :]
+                out_ref[0, r, i, :, lanes] = part.astype(BF16)
 
 
 def last_kernel(pack, width, recv_ref, factor_ref, gating_ref, out_ref, wide_ref):
-    sources, _, groups, rows, _ = recv_ref.shape
+    sources, _, rows, groups, _ = recv_ref.shape
     order = factor_ref.shape[0]
+    widen(pack, width, recv_ref.at[:, 0], wide_ref)
+    left = wide_ref[...].reshape(pack * rows * groups, order)
+    step = 2 * LANES
+    for at in range(0, order, step):
+        mixed = jnp.dot(left, factor_ref[:, at : at + step], preferred_element_type=F32)
+        mixed = mixed.astype(BF16).astype(F32)
+        mixed = mixed.reshape(pack, rows, groups, step)
+        gated = mixed * gating_ref[0, 0, :, :, :, at : at + step].astype(F32)
+        out_ref[0, 0, :, :, :, at : at + step] = gated.astype(BF16)
+
+
+def widen(pack, width, recv, wide_ref):
+    sources, rows, groups, _ = recv.shape
     for t in range(sources // pack):
-        tiles = [
-            recv_ref[t * pack + r, 0].astype(F32).reshape(groups * rows, LANES) for r in range(pack)
-        ]
+        tiles = [recv[t * pack + r].astype(F32).reshape(rows * groups, LANES) for r in range(pack)]
         moved = regroup(tiles, width)
         for q in range(pack):
-            wide_ref[:, q, :, t * LANES : (t + 1) * LANES] = moved[q].astype(BF16).reshape(groups, rows, LANES)
-    left = wide_ref[...].reshape(groups * pack * rows, order)
-    step = 2 * LANES
-    for at in range(0, order, step):
-        mixed = dot_nt(left, factor_ref[at : at + step, :]).astype(BF16)
-        mixed = mixed.reshape(groups * pack, rows, step).astype(F32)
-        gated = mixed * gating_ref[0, :, :, at : at + step].astype(F32)
-        out_ref[0, :, :, at : at + step] = gated.astype(BF16)
+            wide_ref[q, :, t * LANES : (t + 1) * LANES] = moved[q].astype(BF16)
 
 
 def project_kernel(count, *refs):
-    gated_refs, (projection_ref, out_ref, left_ref, right_ref) = refs[:count], refs[count:]
-    parts, channels, rows, step = gated_refs[0].shape
+    gated_refs, (projection_ref, out_ref, turn_ref) = refs[:count], refs[count:]
+    parts, _, pack, rows, _, step = gated_refs[0].shape
     total = projection_ref.shape[0]
     tiles = step // LANES
-    for g, ref in enumerate(gated_refs):
-        for x in range(parts):
-            start = (x * (total // parts) + g * channels) * rows
-            for t in range(tiles):
-                left_ref[t, start : start + channels * rows, :] = (
-                    ref[x, :, :, t * LANES : (t + 1) * LANES].astype(F32).reshape(channels * rows, LANES)
-                )
     for i in range(rows):
         right = jnp.concatenate(
-            [left_ref[t, pl.ds(i, total, stride=rows), :].astype(BF16) for t in range(tiles)], axis=1
+            [
+                ref[x, n, r, i]
+                for x in range(parts)
+                for ref in gated_refs
+                for n in range(ref.shape[1])
+                for r in range(pack)
+            ],
+            axis=0,
         )
         done = jnp.dot(projection_ref[...], right, preferred_element_type=F32)
         for t in range(tiles):
-            right_ref[t, pl.ds(i, total, stride=rows), :] = done[:, t * LANES : (t + 1) * LANES]
+            turn_ref[t, i // SUBLANES, pl.ds(i % SUBLANES, total, stride=SUBLANES), :] = done[
+                :, t * LANES : (t + 1) * LANES
+            ]
+    some = largest_divisor(total, 32)
     for t in range(tiles):
-        out_ref[:, :, t * LANES : (t + 1) * LANES] = right_ref[t].reshape(total, rows, LANES).astype(BF16)
-
-
-def params(grid):
+        for e in range(0, total, some):
+            halves = [
+                turn_ref[t, h, e * SUBLANES : (e + some) * SUBLANES].reshape(some, SUBLANES, LANES)
+                for h in range(rows // SUBLANES)
+            ]
+            out_ref[e : e + some, :, t * LANES : (t + 1) * LANES] = jnp.concatenate(halves, axis=1).astype(BF16)
+
+
+def params(grid, mib):
     return pltpu.CompilerParams(
-        vmem_limit_bytes=VMEM, dimension_semantics=("arbitrary",) * len(grid)
+        vmem_limit_bytes=mib * MIB, dimension_semantics=("arbitrary",) * len(grid)
     )
 
 
@@ -127,7 +154,7 @@
     channels, rows, order = tokens.shape
     width = order // sources
     pack = LANES // width
-    per = pack * largest_divisor(count // pack, 16 // pack)
+    per = pack * largest_divisor(count // pack, FIRST // pack)
     grid = (count // per,)
     return pl.pallas_call(
         partial(first_kernel, pack, width),
@@ -139,7 +166,7 @@
         ],
         out_specs=pl.BlockSpec((sources, per // pack, rows, LANES), lambda n: (0, n, 0, 0)),
         out_shape=jax.ShapeDtypeStruct((sources, count // pack, rows, LANES), BF16),
-        compiler_params=params(grid),
+        compiler_params=params(grid, 60),
         cost_estimate=pl.CostEstimate(
             flops=2 * count * rows * order * order, bytes_accessed=4 * count * rows * order, transcendentals=0
         ),
@@ -147,52 +174,74 @@
     )(tokens, factor, twiddle)
 
 
-def middle_step(received, kernel, second, back, twiddle, at, dests):
-    sources, groups, rows, _ = received.shape
-    channels, width, outer = kernel.shape
+def middle_step(received, kernel, second, back, twiddle, offset, at, count, dests):
+    sources, _, rows, _ = received.shape
+    channels, width, size = kernel.shape
     pack = LANES // width
-    per = largest_divisor(groups, 6)
+    per = GROUPS
+    groups = count // pack
     grid = (groups // per,)
-    out_rows = outer // dests
+    out_rows = size // dests
     return pl.pallas_call(
         partial(middle_kernel, pack),
         grid=grid,
         in_specs=[
-            pl.BlockSpec((sources, per, rows, LANES), lambda n: (0, n, 0, 0)),
-            pl.BlockSpec((per * pack, width, outer), lambda n: (at // (per * pack) + n, 0, 0)),
+            pl.BlockSpec((sources, per, rows, LANES), lambda n: (0, offset // (per * pack) + n, 0, 0)),
+            pl.BlockSpec((per * pack, width, size), lambda n: (at // (per * pack) + n, 0, 0)),
             pl.BlockSpec(second.shape, lambda n: (0, 0)),
             pl.BlockSpec(back.shape, lambda n: (0, 0)),
             pl.BlockSpec(twiddle.shape, lambda n: (0, 0)),
         ],
-        out_specs=pl.BlockSpec((dests, per, out_rows, LANES), lambda n: (0, n, 0, 0)),
-        out_shape=jax.ShapeDtypeStruct((dests, groups, out_rows, LANES), BF16),
-        compiler_params=params(grid),
+        out_specs=pl.BlockSpec((dests, out_rows, per, LANES), lambda n: (0, 0, n, 0)),
+        out_shape=jax.ShapeDtypeStruct((dests, out_rows, groups, LANES), BF16),
+        scratch_shapes=[pltpu.VMEM((size * per, LANES), F32)],
+        compiler_params=params(grid, 32),
         cost_estimate=pl.CostEstimate(
-            flops=4 * groups * LANES * outer * outer, bytes_accessed=6 * groups * LANES * outer, transcendentals=0
+            flops=4 * groups * LANES * size * size, bytes_accessed=6 * groups * LANES * size, transcendentals=0
         ),
         name="outer_factors",
     )(received, kernel, second, back, twiddle)
 
 
+def turn_step(gating, pack):
+    total, rows, order = gating.shape
+    per = GROUPS * pack
+    grid = (total // per,)
+    return pl.pallas_call(
+        partial(turn_kernel, pack),
+        grid=grid,
+        in_specs=[pl.BlockSpec((per, rows, order), lambda n: (n, 0, 0))],
+        out_specs=pl.BlockSpec((1, pack, rows, GROUPS, order), lambda n: (n, 0, 0, 0, 0)),
+        out_shape=jax.ShapeDtypeStruct((total // per, pack, rows, GROUPS, order), BF16),
+        scratch_shapes=[pltpu.VMEM((order // LANES, per * rows, LANES), F32)],
+        compiler_params=params(grid, 32),
+        cost_estimate=pl.CostEstimate(
+            flops=total * rows * order, bytes_accessed=4 * total * rows * order, transcendentals=0
+        ),
+        name="turn_gating",
+    )(gating)
+
+
 def last_step(returned, factor, gating, at, sources):
-    _, parts, groups, rows, _ = returned.shape
+    _, parts, rows, groups, _ = returned.shape
     order = factor.shape[0]
     width = order // sources
     pack = LANES // width
-    per = largest_divisor(groups, 32 // pack)
+    per = GROUPS
     grid = (parts, groups // per)
+    block = (1, 1, pack, rows, per, order)
     return pl.pallas_call(
         partial(last_kernel, pack, width),
         grid=grid,
         in_specs=[
-            pl.BlockSpec((sources, 1, per, rows, LANES), lambda x, n: (0, x, n, 0, 0)),
+            pl.BlockSpec((sources, 1, rows, per, LANES), lambda x, n: (0, x, 0, n, 0)),
             pl.BlockSpec(factor.shape, lambda x, n: (0, 0)),
-            pl.BlockSpec((1, per * pack, rows, order), lambda x, n: (x, at // (per * pack) + n, 0, 0)),
+            pl.BlockSpec(block, lambda x, n: (x, at // (per * pack) + n, 0, 0, 0, 0)),
         ],
-        out_specs=pl.BlockSpec((1, per * pack, rows, order), lambda x, n: (x, n, 0, 0)),
-        out_shape=jax.ShapeDtypeStruct((parts, groups * pack, rows, order), BF16),
-        scratch_shapes=[pltpu.VMEM((per, pack, rows, order), BF16)],
-        compiler_params=params(grid),
+        out_specs=pl.BlockSpec(block, lambda x, n: (x, n, 0, 0, 0, 0)),
+        out_shape=jax.ShapeDtypeStruct((parts, groups // per, pack, rows, per, order), BF16),
+        scratch_shapes=[pltpu.VMEM((pack, rows * per, order), BF16)],
+        compiler_params=params(grid, 32),
         cost_estimate=pl.CostEstimate(
             flops=2 * parts * groups * pack * rows * order * order,
             bytes_accessed=6 * parts * groups * pack * rows * order,
@@ -203,24 +252,35 @@
 
 
 def project_step(gated, projection):
-    parts, channels, rows, order = gated[0].shape
+    _, _, _, rows, _, order = gated[0].shape
     total = projection.shape[0]
     step = 2 * LANES
     grid = (order // step,)
     return pl.pallas_call(
         partial(project_kernel, len(gated)),
         grid=grid,
-        in_specs=[pl.BlockSpec((parts, channels, rows, step), lambda n: (0, 0, 0, n)) for _ in gated]
+        in_specs=[
+            pl.BlockSpec(part.shape[:-1] + (step,), lambda n: (0, 0, 0, 0, 0, n)) for part in gated
+        ]
         + [pl.BlockSpec(projection.shape, lambda n: (0, 0))],
         out_specs=pl.BlockSpec((total, rows, step), lambda n: (0, 0, n)),
         out_shape=jax.ShapeDtypeStruct((total, rows, order), BF16),
-        scratch_shapes=[pltpu.VMEM((step // LANES, total * rows, LANES), F32)] * 2,
-        compiler_params=params(grid),
+        scratch_shapes=[
+            pltpu.VMEM((step // LANES, rows // SUBLANES, total * SUBLANES, LANES), F32),
+        ],
+        compiler_params=params(grid, 28),
         cost_estimate=pl.CostEstimate(
             flops=2 * total * total * rows * order, bytes_accessed=4 * total * rows * order, transcendentals=0
         ),
         name="projection",
     )(*gated, projection)
+
+
+def spans(sizes):
+    at = 0
+    for size in sizes:
+        yield at, size
+        at += size
 
 
 def chunked(
@@ -240,26 +300,40 @@
     channels, _, order = tokens.shape
     width = order // sources
     pack = LANES // width
+    unit = GROUPS * pack
+    units = channels // unit
     total, out_rows, _ = gating.shape
-    gating = gating.reshape(parts, channels, out_rows, order)
+    inverse_first = inverse_first.T
     twiddle_back = jnp.tile(inverse_twiddle.T, (1, pack))
-    projection = projection.T
-    chunks = 4
-    count = channels // chunks
-    received = []
-    for g in range(chunks):
-        sent = first_step(tokens, first_factor, first_twiddle, g * count, count, sources)
-        received.append(lax.all_to_all(sent, "seq", split_axis=0, concat_axis=0, tiled=True))
-    returned = []
-    for g in range(chunks):
+    projection = projection.T.reshape(total, total // unit, GROUPS, pack)
+    projection = projection.transpose(0, 1, 3, 2).reshape(total, total)
+    there = [unit, channels - unit] if units > 1 else [unit]
+    back = [unit, channels - 2 * unit, unit] if units > 2 else [unit] * units
+
+    turned = turn_step(gating, pack).reshape(parts, units, pack, out_rows, GROUPS, order)
+    starts, arrived = [], []
+
+    def exchange(sent, axes):
+        if arrived:
+            sent, arrived[-1] = lax.optimization_barrier((sent, arrived[-1]))
+        arrived.append(lax.all_to_all(sent, axes, split_axis=0, concat_axis=0, tiled=True))
+
+    for at, count in spans(there):
+        starts.append(at)
+        exchange(first_step(tokens, first_factor, first_twiddle, at, count, sources), "seq")
+    for at, count in spans(back):
+        n = max(n for n, start in enumerate(starts) if start <= at)
         sent = middle_step(
-            received[g], kernel, second_factor, inverse_second, twiddle_back, g * count, dests
+            arrived[n], kernel, second_factor, inverse_second, twiddle_back, at - starts[n], at, count, dests
         )
-        returned.append(lax.all_to_all(sent, ("seq", "chan"), split_axis=0, concat_axis=0, tiled=True))
+        if at > 0 and at + count == channels:
+            sent, turned = lax.optimization_barrier((sent, turned))
+        exchange(sent, ("seq", "chan"))
+    returned = arrived[len(there) :]
     gated = []
-    for g in range(chunks):
-        back = returned[g].reshape(sources, parts, count // pack, out_rows, LANES)
-        gated.append(last_step(back, inverse_first, gating, g * count, sources))
+    for (at, count), block in zip(spans(back), returned, strict=True):
+        block = block.reshape(sources, parts, out_rows, count // pack, LANES)
+        gated.append(last_step(block, inverse_first, turned, at, sources))
     return project_step(gated, projection)
 
 
@@ -318,6 +392,7 @@
     tokens, gating = arrays[:2]
     width = tokens.shape[2] // lax.axis_size("seq")
     whole_tiles = gating.shape[1] % 16 == 0 and tokens.shape[1] % 16 == 0 and LANES % width == 0
+    whole_tiles = whole_tiles and tokens.shape[0] % (GROUPS * LANES // width) == 0
     return chunked(*arrays) if whole_tiles else plain(*arrays)
 
 

time: 648 us -> 615 us (0.949)
  waiting for transfers between devices: 475 us -> 437 us
  local copies, waits for them, and re-layouts: 18 us -> 36.3 us
  starting transfers between devices: 47.2 us -> 32.6 us
    all_to_all x8 -> x5, waiting for transfers between devices: 475 us -> 437 us  [exchange(): lax.all_to_all(sent, axes, split_axis=0, concat_axis=0, tiled=True)]
    pallas_call x0 -> x1, Pallas kernels: none -> 19 us  [turn_step(): pl.pallas_call(partial(turn_kernel, pack), grid=grid, in_specs=[pl.BlockS...]
    unnamed x39 -> x33, local copies, waits for them, and re-layouts: 17.9 us -> 34.1 us
    all_to_all x8 -> x5, starting transfers between devices: 47.2 us -> 32.6 us  [exchange(): lax.all_to_all(sent, axes, split_axis=0, concat_axis=0, tiled=True)]
    pallas_call x1, Pallas kernels: 24.2 us -> 13 us  [project_step(): pl.pallas_call(partial(project_kernel, len(gated)), grid=grid, in_specs=[...]
    pallas_call x4 -> x3, Pallas kernels: 24.6 us -> 20.3 us  [last_step(): pl.pallas_call(partial(last_kernel, pack, width), grid=grid, in_specs=[pl...]
    pallas_call x4 -> x3, Pallas kernels: 30.8 us -> 28.8 us  [middle_step(): pl.pallas_call(partial(middle_kernel, pack), grid=grid, in_specs=[pl.Bloc...]
    pallas_call x4 -> x2, Pallas kernels: 22.2 us -> 23.5 us  [first_step(): pl.pallas_call(partial(first_kernel, pack, width), grid=grid, in_specs=[p...]
  transfers between devices with their start and end apart: 8 -> 5, of which waited for: 8 -> 5; matrix products, arithmetic and copies ran while one was open for 0% -> 1% of each run, Pallas kernels for 10% -> 13%
where the time goes in v2:
time: 615 us; the launch traced here: 610 us
  waiting for transfers between devices  437 us (71%)
  Pallas kernels  105 us (17%)
  local copies, waits for them, and re-layouts  36.3 us (6%)
  starting transfers between devices  32.6 us (5%)
    all_to_all x5, waiting for transfers between devices, exchange(): lax.all_to_all(sent, axes, split_axis=0, concat_axis=0, tiled=True)  437 us
    unnamed x33, local copies, waits for them, and re-layouts  34.1 us
    all_to_all x5, starting transfers between devices, exchange(): lax.all_to_all(sent, axes, split_axis=0, concat_axis=0, tiled=True)  32.6 us
    pallas_call x3, Pallas kernels, middle_step(): pl.pallas_call(partial(middle_kernel, pack), grid=grid, in_specs=[pl.Bloc...  28.8 us
    pallas_call x2, Pallas kernels, first_step(): pl.pallas_call(partial(first_kernel, pack, width), grid=grid, in_specs=[p...  23.5 us
    pallas_call x3, Pallas kernels, last_step(): pl.pallas_call(partial(last_kernel, pack, width), grid=grid, in_specs=[pl...  20.3 us
    pallas_call x1, Pallas kernels, turn_step(): pl.pallas_call(partial(turn_kernel, pack), grid=grid, in_specs=[pl.BlockS...  19 us
    pallas_call x1, Pallas kernels, project_step(): pl.pallas_call(partial(project_kernel, len(gated)), grid=grid, in_specs=[...  13 us
  transfers between devices with their start and end apart: 5, of which 5 were waited for; matrix products, arithmetic and copies ran while one was open for 1% of the time, Pallas kernels for 13%

profile of v2, /device:TPU:12, one launch (start us, length us, event | category | flops | bytes accessed | tf_op | source)
XLA Modules:
  0.0 610.2 jit_solution(8034946145959219829)
XLA Ops:
  0.0 5.7 first_factor.3
  5.7 6.2 %all-to-all-start = ((bf16[16,16,32,128]{3,2,1,0:T(8,128)(2,1)}), bf16[16,16,32,128]{3,2,1,0:T(8,128)(2,1)S(1)}, u32[]{:S(2)}, u32[]{:S(2)}) async-start(bf16[16,16,32,128]{3,2,1,0:T(8,128)(2,1)} %first_factor.3), calls=%async_computation | async-start | bytes 4194304 | tf_op jit(solution)/shard_map/all_to_all | solution.py:319
  11.9 17.8 %first_factor.2 = bf16[16,80,32,128]{3,2,1,0:T(8,128)(2,1)} custom-call(bf16[192,32,1024]{2,1,0:T(8,128)(2,1)} %tokens_ref.3, bf16[1024,1024]{1,0:T(8,128)(2,1)} %factor_ref.3, f32[32,1024]{1,0:T(8,128)} %twiddle_ref.3), custom_call_target="tpu_custom_call" | custom-call | flops 10737418240 | bytes 20971520 | tf_op jit(solution)/shard_map/first_factor/pallas_call | solution.py:159
  29.8 29.4 %all-to-all-done.recv_ref = bf16[16,16,32,128]{3,2,1,0:T(8,128)(2,1)S(1)} async-done(((bf16[16,16,32,128]{3,2,1,0:T(8,128)(2,1)}), bf16[16,16,32,128]{3,2,1,0:T(8,128)(2,1)S(1)}, u32[]{:S(2)}, u32[]{:S(2)}) %all-to-all-start) | async-done | bytes 2097184 | tf_op jit(solution)/shard_map/all_to_all | solution.py:319
  59.2 5.1 all-to-all-start.1
  64.2 0.0 copy-done.15
  64.2 0.7 tile.4
  65.0 1.1 copy.19.twiddle_ref
  66.1 0.0 copy-done.12
  66.1 0.0 copy-done.13
  66.1 0.0 copy-start.3
  66.1 4.6 copy-done.3
  70.7 3.4 outer_factors.3
  74.0 0.0 copy-start.9
  74.0 1.3 copy-done.9
  75.4 216.0 %all-to-all-done.1.recv_ref = bf16[16,80,32,128]{3,2,1,0:T(8,128)(2,1)} async-done(((bf16[16,80,32,128]{3,2,1,0:T(8,128)(2,1)}), bf16[16,80,32,128]{3,2,1,0:T(8,128)(2,1)}, u32[]{:S(2)}, u32[]{:S(2)}) %all-to-all-start.1) | async-done | bytes 10485792 | tf_op jit(solution)/shard_map/all_to_all | solution.py:319
  291.4 4.8 all-to-all-start.2
  296.2 18.5 %outer_factors.4 = bf16[32,16,64,128]{3,2,1,0:T(8,128)(2,1)S(1)} custom-call(bf16[16,80,32,128]{3,2,1,0:T(8,128)(2,1)} %all-to-all-done.1.recv_ref, bf16[192,64,512]{2,1,0:T(8,128)(2,1)} %kernel_ref.5, bf16[512,512]{1,0:T(8,128)(2,1)S(1)} %copy-done.12, bf16[512,512]{1,0:T(8,128)(2,1)S(1)} %copy-done.13, f32[512,128]{1,0:T(8,128)S(1)} %copy.19.twiddle_ref), custom_call_target="tpu_custom_call" | custom-call | flops 8589934592 | bytes 25165824 | tf_op jit(solution)/shard_map/outer_factors/pallas_call | solution.py:185
  314.7 0.0 copy-start.4
  314.7 3.4 copy-done.4
  318.1 24.7 %all-to-all-done.2 = bf16[32,16,16,128]{3,2,1,0:T(8,128)(2,1)S(1)} async-done(((bf16[32,16,16,128]{3,2,1,0:T(8,128)(2,1)}), bf16[32,16,16,128]{3,2,1,0:T(8,128)(2,1)S(1)}, u32[]{:S(2)}, u32[]{:S(2)}) %all-to-all-start.2) | async-done | bytes 2097184 | tf_op jit(solution)/shard_map/all_to_all | solution.py:319
  342.8 1.3 copy-done.7
  344.1 5.9 all-to-all-start.3
  350.0 19.0 %turn_gating.1 = bf16[12,2,16,16,1024]{4,3,2,1,0:T(8,128)(2,1)S(1)} custom-call(bf16[384,16,1024]{2,1,0:T(8,128)(2,1)} %gating_ref.1), custom_call_target="tpu_custom_call" | custom-call | flops 6291456 | bytes 25165824 | tf_op jit(solution)/shard_map/turn_gating/pallas_call | solution.py:210
  369.0 0.0 copy-start
  369.0 4.8 copy-done
  373.8 6.9 %outer_factors.5 = bf16[32,16,16,128]{3,2,1,0:T(8,128)(2,1)} custom-call(bf16[16,80,32,128]{3,2,1,0:T(8,128)(2,1)} %all-to-all-done.1.recv_ref, bf16[192,64,512]{2,1,0:T(8,128)(2,1)} %kernel_ref.5, bf16[512,512]{1,0:T(8,128)(2,1)S(1)} %copy-done.12, bf16[512,512]{1,0:T(8,128)(2,1)S(1)} %copy-done.13, f32[512,128]{1,0:T(8,128)S(1)} %copy.19.twiddle_ref), custom_call_target="tpu_custom_call" | custom-call | flops 2147483648 | bytes 6291456 | tf_op jit(solution)/shard_map/outer_factors/pallas_call | solution.py:185
  380.7 150.0 %all-to-all-done.3 = bf16[32,16,64,128]{3,2,1,0:T(8,128)(2,1)} async-done(((bf16[32,16,64,128]{3,2,1,0:T(8,128)(2,1)}), bf16[32,16,64,128]{3,2,1,0:T(8,128)(2,1)}, u32[]{:S(2)}, u32[]{:S(2)}) %all-to-all-start.3) | async-done | bytes 8388640 | tf_op jit(solution)/shard_map/all_to_all | solution.py:319
  530.7 10.6 %all-to-all-start.4 = ((bf16[32,16,16,128]{3,2,1,0:T(8,128)(2,1)}), bf16[32,16,16,128]{3,2,1,0:T(8,128)(2,1)}, u32[]{:S(2)}, u32[]{:S(2)}) async-start(bf16[32,16,16,128]{3,2,1,0:T(8,128)(2,1)} %outer_factors.5), calls=%async_computation.4 | async-start | bytes 4194304 | tf_op jit(solution)/shard_map/all_to_all | solution.py:319
  541.4 0.0 copy-start.14
  541.4 2.9 copy.21
  544.3 0.0 copy-done.14
  544.3 0.1 reshape.26
  544.5 0.2 copy.24.refs_3_
  544.7 0.0 copy-start.1
  544.7 4.6 copy-done.1
  549.3 1.6 copy-done.8
  550.9 2.9 last_factor.3.refs_0_
  553.8 0.0 copy-start.5
  553.8 1.3 copy-done.5
  555.1 13.3 %last_factor.4.refs_1_ = bf16[2,4,2,16,16,1024]{5,4,3,2,1,0:T(8,128)(2,1)S(1)} custom-call(bf16[16,2,16,64,128]{4,3,2,1,0:T(8,128)(2,1)} %bitcast.5.recv_ref, bf16[1024,1024]{1,0:T(8,128)(2,1)S(1)} %bitcast.16, bf16[2,6,2,16,16,1024]{5,4,3,2,1,0:T(8,128)(2,1)} %bitcast.12), custom_call_target="tpu_custom_call" | custom-call | flops 8589934592 | bytes 25165824 | tf_op jit(solution)/shard_map/last_factor/pallas_call | solution.py:233
  568.3 0.0 copy-start.10
  568.3 3.3 copy-done.10
  571.6 16.4 %all-to-all-done.4 = bf16[32,16,16,128]{3,2,1,0:T(8,128)(2,1)} async-done(((bf16[32,16,16,128]{3,2,1,0:T(8,128)(2,1)}), bf16[32,16,16,128]{3,2,1,0:T(8,128)(2,1)}, u32[]{:S(2)}, u32[]{:S(2)}) %all-to-all-start.4) | async-done | bytes 2097184 | tf_op jit(solution)/shard_map/all_to_all | solution.py:319
  588.0 4.6 copy-done.2
  592.6 4.1 last_factor.5.refs_2_
  596.8 0.5 copy-done.11
  597.3 13.0 %projection.1 = bf16[384,16,1024]{2,1,0:T(8,128)(2,1)} custom-call(bf16[2,1,2,16,16,1024]{5,4,3,2,1,0:T(8,128)(2,1)S(1)} %copy-done.6, bf16[2,4,2,16,16,1024]{5,4,3,2,1,0:T(8,128)(2,1)S(1)} %copy-done.11, bf16[2,1,2,16,16,1024]{5,4,3,2,1,0:T(8,128)(2,1)S(1)} %last_factor.5.refs_2_, bf16[384,384]{1,0:T(8,128)(2,1)S(1)} %copy.24.refs_3_), custom_call_target="tpu_custom_call" | custom-call | flops 4831838208 | bytes 25165824 | tf_op jit(solution)/shard_map/projection/pallas_call | solution.py:259
  (10 shorter events, 0.1 us)
Async XLA Ops:
  5.7 53.5 %all-to-all-start = ((bf16[16,16,32,128]{3,2,1,0:T(8,128)(2,1)}), bf16[16,16,32,128]{3,2,1,0:T(8,128)(2,1)S(1)}, u32[]{:S(2)}, u32[]{:S(2)}) async-start(bf16[16,16,32,128]{3,2,1,0:T(8,128)(2,1)} %first_factor.3), calls=%async_computation | async-start | bytes 4194304 | tf_op jit(solution)/shard_map/all_to_all | solution.py:319
  29.7 34.5 %copy-start.15 = (f32[64,512]{1,0:T(8,128)S(1)}, f32[64,512]{1,0:T(8,128)}, u32[]{:S(2)}) copy-start(f32[64,512]{1,0:T(8,128)} %param.17) | copy-start | bytes 393220
  29.7 36.3 %copy-start.12 = (bf16[512,512]{1,0:T(8,128)(2,1)S(1)}, bf16[512,512]{1,0:T(8,128)(2,1)}, u32[]{:S(2)}) copy-start(bf16[512,512]{1,0:T(8,128)(2,1)} %second_ref.5) | copy-start | bytes 1572868
  29.8 36.3 %copy-start.13 = (bf16[512,512]{1,0:T(8,128)(2,1)S(1)}, bf16[512,512]{1,0:T(8,128)(2,1)}, u32[]{:S(2)}) copy-start(bf16[512,512]{1,0:T(8,128)(2,1)} %back_ref.5) | copy-start | bytes 1572868
  59.2 232.2 %all-to-all-start.1 = ((bf16[16,80,32,128]{3,2,1,0:T(8,128)(2,1)}), bf16[16,80,32,128]{3,2,1,0:T(8,128)(2,1)}, u32[]{:S(2)}, u32[]{:S(2)}) async-start(bf16[16,80,32,128]{3,2,1,0:T(8,128)(2,1)} %first_factor.2), calls=%async_computation.1 | async-start | bytes 20971520 | tf_op jit(solution)/shard_map/all_to_all | solution.py:319
  66.1 4.6 copy-start.3
  74.0 1.3 copy-start.9
  291.4 51.4 %all-to-all-start.2 = ((bf16[32,16,16,128]{3,2,1,0:T(8,128)(2,1)}), bf16[32,16,16,128]{3,2,1,0:T(8,128)(2,1)S(1)}, u32[]{:S(2)}, u32[]{:S(2)}) async-start(bf16[32,16,16,128]{3,2,1,0:T(8,128)(2,1)} %copy-done.9), calls=%async_computation.2 | async-start | bytes 4194304 | tf_op jit(solution)/shard_map/all_to_all | solution.py:319
  314.7 3.4 copy-start.4
  342.8 1.3 copy-start.7
  344.1 186.6 %all-to-all-start.3 = ((bf16[32,16,64,128]{3,2,1,0:T(8,128)(2,1)}), bf16[32,16,64,128]{3,2,1,0:T(8,128)(2,1)}, u32[]{:S(2)}, u32[]{:S(2)}) async-start(bf16[32,16,64,128]{3,2,1,0:T(8,128)(2,1)} %copy-done.4), calls=%async_computation.3 | async-start | bytes 16777216 | tf_op jit(solution)/shard_map/all_to_all | solution.py:319
  369.0 4.8 copy-start
  530.7 57.3 %all-to-all-start.4 = ((bf16[32,16,16,128]{3,2,1,0:T(8,128)(2,1)}), bf16[32,16,16,128]{3,2,1,0:T(8,128)(2,1)}, u32[]{:S(2)}, u32[]{:S(2)}) async-start(bf16[32,16,16,128]{3,2,1,0:T(8,128)(2,1)} %outer_factors.5), calls=%async_computation.4 | async-start | bytes 4194304 | tf_op jit(solution)/shard_map/all_to_all | solution.py:319
  541.4 2.9 copy-start.14
  544.7 4.6 copy-start.1
  549.3 1.6 copy-start.8
  553.8 1.3 copy-start.5
  568.3 3.3 copy-start.10
  588.0 4.6 copy-start.2
  592.6 4.1 copy-start.6
  592.6 4.7 copy-start.11

commit v3 on v2

--- a/solution.py
+++ b/solution.py
@@ -79,15 +79,15 @@
 
 
 def turn_kernel(pack, gating_ref, out_ref, turn_ref):
-    channels, rows, order = gating_ref.shape
+    _, channels, rows, order = gating_ref.shape
     groups = channels // pack
     for t in range(order // LANES):
         lanes = slice(t * LANES, (t + 1) * LANES)
-        turn_ref[t] = gating_ref[:, :, lanes].astype(F32).reshape(channels * rows, LANES)
+        turn_ref[t] = gating_ref[0, :, :, lanes].astype(F32).reshape(channels * rows, LANES)
         for r in range(pack):
             for i in range(rows):
                 part = turn_ref[t, pl.ds(r * rows + i, groups, stride=pack * rows), :]
-                out_ref[0, r, i, :, lanes] = part.astype(BF16)
+                out_ref[0, 0, r, i, :, lanes] = part.astype(BF16)
 
 
 def last_kernel(pack, width, recv_ref, factor_ref, gating_ref, out_ref, wide_ref):
@@ -203,26 +203,26 @@
     )(received, kernel, second, back, twiddle)
 
 
-def turn_step(gating, pack):
-    total, rows, order = gating.shape
+def turn_step(gating, pack, at, count):
+    parts, _, rows, order = gating.shape
     per = GROUPS * pack
-    grid = (total // per,)
+    grid = (parts, count // per)
     return pl.pallas_call(
         partial(turn_kernel, pack),
         grid=grid,
-        in_specs=[pl.BlockSpec((per, rows, order), lambda n: (n, 0, 0))],
-        out_specs=pl.BlockSpec((1, pack, rows, GROUPS, order), lambda n: (n, 0, 0, 0, 0)),
-        out_shape=jax.ShapeDtypeStruct((total // per, pack, rows, GROUPS, order), BF16),
+        in_specs=[pl.BlockSpec((1, per, rows, order), lambda x, n: (x, at // per + n, 0, 0))],
+        out_specs=pl.BlockSpec((1, 1, pack, rows, GROUPS, order), lambda x, n: (x, n, 0, 0, 0, 0)),
+        out_shape=jax.ShapeDtypeStruct((parts, count // per, pack, rows, GROUPS, order), BF16),
         scratch_shapes=[pltpu.VMEM((order // LANES, per * rows, LANES), F32)],
         compiler_params=params(grid, 32),
         cost_estimate=pl.CostEstimate(
-            flops=total * rows * order, bytes_accessed=4 * total * rows * order, transcendentals=0
+            flops=parts * count * rows * order, bytes_accessed=4 * parts * count * rows * order, transcendentals=0
         ),
         name="turn_gating",
     )(gating)
 
 
-def last_step(returned, factor, gating, at, sources):
+def last_step(returned, factor, gating, sources):
     _, parts, rows, groups, _ = returned.shape
     order = factor.shape[0]
     width = order // sources
@@ -236,7 +236,7 @@
         in_specs=[
             pl.BlockSpec((sources, 1, rows, per, LANES), lambda x, n: (0, x, 0, n, 0)),
             pl.BlockSpec(factor.shape, lambda x, n: (0, 0)),
-            pl.BlockSpec(block, lambda x, n: (x, at // (per * pack) + n, 0, 0, 0, 0)),
+            pl.BlockSpec(block, lambda x, n: (x, n, 0, 0, 0, 0)),
         ],
         out_specs=pl.BlockSpec(block, lambda x, n: (x, n, 0, 0, 0, 0)),
         out_shape=jax.ShapeDtypeStruct((parts, groups // per, pack, rows, per, order), BF16),
@@ -310,7 +310,8 @@
     there = [unit, channels - unit] if units > 1 else [unit]
     back = [unit, channels - 2 * unit, unit] if units > 2 else [unit] * units
 
-    turned = turn_step(gating, pack).reshape(parts, units, pack, out_rows, GROUPS, order)
+    gating = gating.reshape(parts, channels, out_rows, order)
+    turned = [turn_step(gating, pack, at, count) for at, count in spans(back)]
     starts, arrived = [], []
 
     def exchange(sent, axes):
@@ -331,9 +332,9 @@
         exchange(sent, ("seq", "chan"))
     returned = arrived[len(there) :]
     gated = []
-    for (at, count), block in zip(spans(back), returned, strict=True):
+    for count, block, gate in zip(back, returned, turned, strict=True):
         block = block.reshape(sources, parts, out_rows, count // pack, LANES)
-        gated.append(last_step(block, inverse_first, turned, at, sources))
+        gated.append(last_step(block, inverse_first, gate, sources))
     return project_step(gated, projection)
 
 

time: 615 us -> 613 us (level)
    pallas_call x1 -> x3, Pallas kernels: 19 us -> 17.7 us  [turn_step(): pl.pallas_call(partial(turn_kernel, pack), grid=grid, in_specs=[pl.BlockS...]
    unnamed x33 -> x39, local copies, waits for them, and re-layouts: 34.1 us -> 35.1 us
where the time goes in v3:
time: 613 us; the launch traced here: 608 us
  waiting for transfers between devices  435 us (71%)
  Pallas kernels  103 us (17%)
  local copies, waits for them, and re-layouts  37.3 us (6%)
  starting transfers between devices  32.6 us (5%)
    all_to_all x5, waiting for transfers between devices, exchange(): lax.all_to_all(sent, axes, split_axis=0, concat_axis=0, tiled=True)  435 us
    unnamed x39, local copies, waits for them, and re-layouts  35.1 us
    all_to_all x5, starting transfers between devices, exchange(): lax.all_to_all(sent, axes, split_axis=0, concat_axis=0, tiled=True)  32.6 us
    pallas_call x3, Pallas kernels, middle_step(): pl.pallas_call(partial(middle_kernel, pack), grid=grid, in_specs=[pl.Bloc...  28.8 us
    pallas_call x2, Pallas kernels, first_step(): pl.pallas_call(partial(first_kernel, pack, width), grid=grid, in_specs=[p...  23.5 us
    pallas_call x3, Pallas kernels, last_step(): pl.pallas_call(partial(last_kernel, pack, width), grid=grid, in_specs=[pl...  20.3 us
    pallas_call x3, Pallas kernels, turn_step(): pl.pallas_call(partial(turn_kernel, pack), grid=grid, in_specs=[pl.BlockS...  17.7 us
    pallas_call x1, Pallas kernels, project_step(): pl.pallas_call(partial(project_kernel, len(gated)), grid=grid, in_specs=[...  13 us
  transfers between devices with their start and end apart: 5, of which 5 were waited for; matrix products, arithmetic and copies ran while one was open for 1% of the time, Pallas kernels for 13%

profile of v3, /device:TPU:12, one launch (start us, length us, event | category | flops | bytes accessed | tf_op | source)
XLA Modules:
  0.0 608.4 jit_solution(15466357475543645577)
XLA Ops:
  0.0 5.7 first_factor.3
  5.7 6.2 %all-to-all-start = ((bf16[16,16,32,128]{3,2,1,0:T(8,128)(2,1)}), bf16[16,16,32,128]{3,2,1,0:T(8,128)(2,1)S(1)}, u32[]{:S(2)}, u32[]{:S(2)}) async-start(bf16[16,16,32,128]{3,2,1,0:T(8,128)(2,1)} %first_factor.3), calls=%async_computation | async-start | bytes 4194304 | tf_op jit(solution)/shard_map/all_to_all | solution.py:320
  12.0 17.8 %first_factor.2 = bf16[16,80,32,128]{3,2,1,0:T(8,128)(2,1)} custom-call(bf16[192,32,1024]{2,1,0:T(8,128)(2,1)} %tokens_ref.3, bf16[1024,1024]{1,0:T(8,128)(2,1)} %factor_ref.3, f32[32,1024]{1,0:T(8,128)} %twiddle_ref.3), custom_call_target="tpu_custom_call" | custom-call | flops 10737418240 | bytes 20971520 | tf_op jit(solution)/shard_map/first_factor/pallas_call | solution.py:159
  29.8 29.4 %all-to-all-done.recv_ref = bf16[16,16,32,128]{3,2,1,0:T(8,128)(2,1)S(1)} async-done(((bf16[16,16,32,128]{3,2,1,0:T(8,128)(2,1)}), bf16[16,16,32,128]{3,2,1,0:T(8,128)(2,1)S(1)}, u32[]{:S(2)}, u32[]{:S(2)}) %all-to-all-start) | async-done | bytes 2097184 | tf_op jit(solution)/shard_map/all_to_all | solution.py:320
  59.2 5.1 all-to-all-start.1
  64.3 0.0 copy-done.18
  64.3 0.7 tile.4
  65.0 1.1 copy.19.twiddle_ref
  66.1 0.0 copy-done.15
  66.1 0.0 copy-start.1
  66.1 4.6 copy-done.1
  70.7 3.4 outer_factors.3
  74.1 1.3 copy-done.3
  75.4 216.0 %all-to-all-done.1.recv_ref = bf16[16,80,32,128]{3,2,1,0:T(8,128)(2,1)} async-done(((bf16[16,80,32,128]{3,2,1,0:T(8,128)(2,1)}), bf16[16,80,32,128]{3,2,1,0:T(8,128)(2,1)}, u32[]{:S(2)}, u32[]{:S(2)}) %all-to-all-start.1) | async-done | bytes 10485792 | tf_op jit(solution)/shard_map/all_to_all | solution.py:320
  291.4 4.8 all-to-all-start.2
  296.2 18.5 %outer_factors.4 = bf16[32,16,64,128]{3,2,1,0:T(8,128)(2,1)S(1)} custom-call(bf16[16,80,32,128]{3,2,1,0:T(8,128)(2,1)} %all-to-all-done.1.recv_ref, bf16[192,64,512]{2,1,0:T(8,128)(2,1)} %kernel_ref.5, bf16[512,512]{1,0:T(8,128)(2,1)S(1)} %copy-done.15, bf16[512,512]{1,0:T(8,128)(2,1)S(1)} %copy-done.16, f32[512,128]{1,0:T(8,128)S(1)} %copy.19.twiddle_ref), custom_call_target="tpu_custom_call" | custom-call | flops 8589934592 | bytes 25165824 | tf_op jit(solution)/shard_map/outer_factors/pallas_call | solution.py:185
  314.7 0.0 copy-start.2
  314.8 3.4 copy-done.2
  318.1 24.7 %all-to-all-done.2 = bf16[32,16,16,128]{3,2,1,0:T(8,128)(2,1)S(1)} async-done(((bf16[32,16,16,128]{3,2,1,0:T(8,128)(2,1)}), bf16[32,16,16,128]{3,2,1,0:T(8,128)(2,1)S(1)}, u32[]{:S(2)}, u32[]{:S(2)}) %all-to-all-start.2) | async-done | bytes 2097184 | tf_op jit(solution)/shard_map/all_to_all | solution.py:320
  342.8 1.3 copy-done.13
  344.1 5.9 all-to-all-start.3
  350.0 0.0 copy-start
  350.0 4.6 copy-done
  354.6 3.0 turn_gating.3.gating_ref
  357.6 1.3 copy-done.9
  358.9 3.0 turn_gating.5.gating_ref
  361.8 1.3 copy-done.7
  363.2 11.8 %turn_gating.4.gating_ref = bf16[2,4,2,16,16,1024]{5,4,3,2,1,0:T(8,128)(2,1)S(1)} custom-call(bf16[2,192,16,1024]{3,2,1,0:T(8,128)(2,1)S(1)} %bitcast.14), custom_call_target="tpu_custom_call" | custom-call | flops 4194304 | bytes 16777216 | tf_op jit(solution)/shard_map/turn_gating/pallas_call | solution.py:210
  375.0 3.4 copy-done.4
  378.4 6.9 %outer_factors.5 = bf16[32,16,16,128]{3,2,1,0:T(8,128)(2,1)} custom-call(bf16[16,80,32,128]{3,2,1,0:T(8,128)(2,1)} %all-to-all-done.1.recv_ref, bf16[192,64,512]{2,1,0:T(8,128)(2,1)} %kernel_ref.5, bf16[512,512]{1,0:T(8,128)(2,1)S(1)} %copy-done.15, bf16[512,512]{1,0:T(8,128)(2,1)S(1)} %copy-done.16, f32[512,128]{1,0:T(8,128)S(1)} %copy.19.twiddle_ref), custom_call_target="tpu_custom_call" | custom-call | flops 2147483648 | bytes 6291456 | tf_op jit(solution)/shard_map/outer_factors/pallas_call | solution.py:185
  385.3 145.5 %all-to-all-done.3 = bf16[32,16,64,128]{3,2,1,0:T(8,128)(2,1)} async-done(((bf16[32,16,64,128]{3,2,1,0:T(8,128)(2,1)}), bf16[32,16,64,128]{3,2,1,0:T(8,128)(2,1)}, u32[]{:S(2)}, u32[]{:S(2)}) %all-to-all-start.3) | async-done | bytes 8388640 | tf_op jit(solution)/shard_map/all_to_all | solution.py:320
  530.8 10.6 %all-to-all-start.4 = ((bf16[32,16,16,128]{3,2,1,0:T(8,128)(2,1)}), bf16[32,16,16,128]{3,2,1,0:T(8,128)(2,1)}, u32[]{:S(2)}, u32[]{:S(2)}) async-start(bf16[32,16,16,128]{3,2,1,0:T(8,128)(2,1)} %outer_factors.5), calls=%async_computation.4 | async-start | bytes 4194304 | tf_op jit(solution)/shard_map/all_to_all | solution.py:320
  541.4 0.0 copy-start.17
  541.4 2.9 copy.21
  544.4 0.1 reshape.26
  544.5 0.2 copy.24.refs_3_
  544.8 1.6 copy-done.10
  546.3 1.6 copy-done.14
  547.9 2.9 last_factor.3.refs_0_
  550.8 1.3 copy-done.11
  552.1 13.2 %last_factor.4.refs_1_ = bf16[2,4,2,16,16,1024]{5,4,3,2,1,0:T(8,128)(2,1)S(1)} custom-call(bf16[16,2,16,64,128]{4,3,2,1,0:T(8,128)(2,1)} %bitcast.5.recv_ref, bf16[1024,1024]{1,0:T(8,128)(2,1)S(1)} %bitcast.16, bf16[2,4,2,16,16,1024]{5,4,3,2,1,0:T(8,128)(2,1)} %copy-done.4), custom_call_target="tpu_custom_call" | custom-call | flops 8589934592 | bytes 25165824 | tf_op jit(solution)/shard_map/last_factor/pallas_call | solution.py:233
  565.4 0.0 copy-start.5
  565.4 3.4 copy-done.5
  568.8 19.3 %all-to-all-done.4 = bf16[32,16,16,128]{3,2,1,0:T(8,128)(2,1)} async-done(((bf16[32,16,16,128]{3,2,1,0:T(8,128)(2,1)}), bf16[32,16,16,128]{3,2,1,0:T(8,128)(2,1)}, u32[]{:S(2)}, u32[]{:S(2)}) %all-to-all-start.4) | async-done | bytes 2097184 | tf_op jit(solution)/shard_map/all_to_all | solution.py:320
  588.1 1.6 copy-done.8
  589.7 4.1 last_factor.5.refs_2_
  593.8 1.6 copy-done.12
  595.4 13.0 %projection.1 = bf16[384,16,1024]{2,1,0:T(8,128)(2,1)} custom-call(bf16[2,1,2,16,16,1024]{5,4,3,2,1,0:T(8,128)(2,1)S(1)} %copy-done.12, bf16[2,4,2,16,16,1024]{5,4,3,2,1,0:T(8,128)(2,1)S(1)} %copy-done.6, bf16[2,1,2,16,16,1024]{5,4,3,2,1,0:T(8,128)(2,1)S(1)} %last_factor.5.refs_2_, bf16[384,384]{1,0:T(8,128)(2,1)S(1)} %copy.24.refs_3_), custom_call_target="tpu_custom_call" | custom-call | flops 4831838208 | bytes 25165824 | tf_op jit(solution)/shard_map/projection/pallas_call | solution.py:259
  (18 shorter events, 0.1 us)
Async XLA Ops:
  5.7 53.5 %all-to-all-start = ((bf16[16,16,32,128]{3,2,1,0:T(8,128)(2,1)}), bf16[16,16,32,128]{3,2,1,0:T(8,128)(2,1)S(1)}, u32[]{:S(2)}, u32[]{:S(2)}) async-start(bf16[16,16,32,128]{3,2,1,0:T(8,128)(2,1)} %first_factor.3), calls=%async_computation | async-start | bytes 4194304 | tf_op jit(solution)/shard_map/all_to_all | solution.py:320
  29.8 34.5 %copy-start.18 = (f32[64,512]{1,0:T(8,128)S(1)}, f32[64,512]{1,0:T(8,128)}, u32[]{:S(2)}) copy-start(f32[64,512]{1,0:T(8,128)} %param.17) | copy-start | bytes 393220
  29.8 36.3 %copy-start.15 = (bf16[512,512]{1,0:T(8,128)(2,1)S(1)}, bf16[512,512]{1,0:T(8,128)(2,1)}, u32[]{:S(2)}) copy-start(bf16[512,512]{1,0:T(8,128)(2,1)} %second_ref.5) | copy-start | bytes 1572868
  29.8 36.3 %copy-start.16 = (bf16[512,512]{1,0:T(8,128)(2,1)S(1)}, bf16[512,512]{1,0:T(8,128)(2,1)}, u32[]{:S(2)}) copy-start(bf16[512,512]{1,0:T(8,128)(2,1)} %back_ref.5) | copy-start | bytes 1572868
  59.2 232.2 %all-to-all-start.1 = ((bf16[16,80,32,128]{3,2,1,0:T(8,128)(2,1)}), bf16[16,80,32,128]{3,2,1,0:T(8,128)(2,1)}, u32[]{:S(2)}, u32[]{:S(2)}) async-start(bf16[16,80,32,128]{3,2,1,0:T(8,128)(2,1)} %first_factor.2), calls=%async_computation.1 | async-start | bytes 20971520 | tf_op jit(solution)/shard_map/all_to_all | solution.py:320
  66.1 4.6 copy-start.1
  74.1 1.3 copy-start.3
  291.4 51.4 %all-to-all-start.2 = ((bf16[32,16,16,128]{3,2,1,0:T(8,128)(2,1)}), bf16[32,16,16,128]{3,2,1,0:T(8,128)(2,1)S(1)}, u32[]{:S(2)}, u32[]{:S(2)}) async-start(bf16[32,16,16,128]{3,2,1,0:T(8,128)(2,1)} %copy-done.3), calls=%async_computation.2 | async-start | bytes 4194304 | tf_op jit(solution)/shard_map/all_to_all | solution.py:320
  314.7 3.4 copy-start.2
  342.8 1.3 copy-start.13
  344.1 186.6 %all-to-all-start.3 = ((bf16[32,16,64,128]{3,2,1,0:T(8,128)(2,1)}), bf16[32,16,64,128]{3,2,1,0:T(8,128)(2,1)}, u32[]{:S(2)}, u32[]{:S(2)}) async-start(bf16[32,16,64,128]{3,2,1,0:T(8,128)(2,1)} %copy-done.2), calls=%async_computation.3 | async-start | bytes 16777216 | tf_op jit(solution)/shard_map/all_to_all | solution.py:320
  350.0 4.6 copy-start
  357.6 1.3 copy-start.9
  361.8 1.4 copy-start.7
  375.0 3.4 copy-start.4
  530.8 57.3 %all-to-all-start.4 = ((bf16[32,16,16,128]{3,2,1,0:T(8,128)(2,1)}), bf16[32,16,16,128]{3,2,1,0:T(8,128)(2,1)}, u32[]{:S(2)}, u32[]{:S(2)}) async-start(bf16[32,16,16,128]{3,2,1,0:T(8,128)(2,1)} %outer_factors.5), calls=%async_computation.4 | async-start | bytes 4194304 | tf_op jit(solution)/shard_map/all_to_all | solution.py:320
  541.4 2.9 copy-start.17
  544.7 1.6 copy-start.10
  546.3 1.6 copy-start.14
  550.8 1.3 copy-start.11
  565.4 3.4 copy-start.5
  588.1 1.6 copy-start.8
  589.6 4.2 copy-start.6
  593.8 1.6 copy-start.12

commit v4 on v3

--- a/solution.py
+++ b/solution.py
@@ -315,7 +315,7 @@
     starts, arrived = [], []
 
     def exchange(sent, axes):
-        if arrived:
+        if arrived and len(arrived) != len(there) + 1:
             sent, arrived[-1] = lax.optimization_barrier((sent, arrived[-1]))
         arrived.append(lax.all_to_all(sent, axes, split_axis=0, concat_axis=0, tiled=True))
 

time: 613 us -> 627 us (1.023)
  blocking collectives: 0 us -> 187 us
  waiting for transfers between devices: 435 us -> 272 us
  starting transfers between devices: 32.6 us -> 22.4 us
    all_to_all x0 -> x1, blocking collectives: none -> 187 us  [exchange(): lax.all_to_all(sent, axes, split_axis=0, concat_axis=0, tiled=True)]
    all_to_all x5 -> x4, waiting for transfers between devices: 435 us -> 272 us  [exchange(): lax.all_to_all(sent, axes, split_axis=0, concat_axis=0, tiled=True)]
    all_to_all x5 -> x4, starting transfers between devices: 32.6 us -> 22.4 us  [exchange(): lax.all_to_all(sent, axes, split_axis=0, concat_axis=0, tiled=True)]
    unnamed x39 -> x37, local copies, waits for them, and re-layouts: 35.1 us -> 33.9 us
  transfers between devices with their start and end apart: 5 -> 4, of which waited for: 5 -> 4; matrix products, arithmetic and copies ran while one was open for 1% -> 1% of each run, Pallas kernels for 13% -> 10%
where the time goes in v4:
time: 627 us; the launch traced here: 623 us
  waiting for transfers between devices  272 us (43%)
  blocking collectives  187 us (30%)
  Pallas kernels  105 us (17%)
  local copies, waits for them, and re-layouts  36 us (6%)
  starting transfers between devices  22.4 us (4%)
    all_to_all x4, waiting for transfers between devices, exchange(): lax.all_to_all(sent, axes, split_axis=0, concat_axis=0, tiled=True)  272 us
    all_to_all x1, blocking collectives, exchange(): lax.all_to_all(sent, axes, split_axis=0, concat_axis=0, tiled=True)  187 us
    unnamed x37, local copies, waits for them, and re-layouts  33.9 us
    pallas_call x3, Pallas kernels, middle_step(): pl.pallas_call(partial(middle_kernel, pack), grid=grid, in_specs=[pl.Bloc...  30.2 us
    pallas_call x2, Pallas kernels, first_step(): pl.pallas_call(partial(first_kernel, pack, width), grid=grid, in_specs=[p...  23.5 us
    all_to_all x4, starting transfers between devices, exchange(): lax.all_to_all(sent, axes, split_axis=0, concat_axis=0, tiled=True)  22.4 us
    pallas_call x3, Pallas kernels, last_step(): pl.pallas_call(partial(last_kernel, pack, width), grid=grid, in_specs=[pl...  20.3 us
    pallas_call x3, Pallas kernels, turn_step(): pl.pallas_call(partial(turn_kernel, pack), grid=grid, in_specs=[pl.BlockS...  17.7 us
  transfers between devices with their start and end apart: 4, of which 4 were waited for; matrix products, arithmetic and copies ran while one was open for 1% of the time, Pallas kernels for 10%

profile of v4, /device:TPU:12, one launch (start us, length us, event | category | flops | bytes accessed | tf_op | source)
XLA Modules:
  0.0 622.6 jit_solution(3160590820974879074)
XLA Ops:
  0.0 5.7 first_factor.3
  5.7 6.2 %all-to-all-start = ((bf16[16,16,32,128]{3,2,1,0:T(8,128)(2,1)}), bf16[16,16,32,128]{3,2,1,0:T(8,128)(2,1)S(1)}, u32[]{:S(2)}, u32[]{:S(2)}) async-start(bf16[16,16,32,128]{3,2,1,0:T(8,128)(2,1)} %first_factor.3), calls=%async_computation | async-start | bytes 4194304 | tf_op jit(solution)/shard_map/all_to_all | solution.py:320
  11.9 17.8 %first_factor.2 = bf16[16,80,32,128]{3,2,1,0:T(8,128)(2,1)} custom-call(bf16[192,32,1024]{2,1,0:T(8,128)(2,1)} %tokens_ref.3, bf16[1024,1024]{1,0:T(8,128)(2,1)} %factor_ref.3, f32[32,1024]{1,0:T(8,128)} %twiddle_ref.3), custom_call_target="tpu_custom_call" | custom-call | flops 10737418240 | bytes 20971520 | tf_op jit(solution)/shard_map/first_factor/pallas_call | solution.py:159
  29.8 29.4 %all-to-all-done.recv_ref = bf16[16,16,32,128]{3,2,1,0:T(8,128)(2,1)S(1)} async-done(((bf16[16,16,32,128]{3,2,1,0:T(8,128)(2,1)}), bf16[16,16,32,128]{3,2,1,0:T(8,128)(2,1)S(1)}, u32[]{:S(2)}, u32[]{:S(2)}) %all-to-all-start) | async-done | bytes 2097184 | tf_op jit(solution)/shard_map/all_to_all | solution.py:320
  59.2 5.1 all-to-all-start.1
  64.2 0.7 tile.4
  65.0 1.1 copy.19.twiddle_ref
  66.1 0.0 copy-start.1
  66.1 4.6 copy-done.1
  70.7 4.8 outer_factors.3
  75.4 216.0 %all-to-all-done.1.recv_ref = bf16[16,80,32,128]{3,2,1,0:T(8,128)(2,1)} async-done(((bf16[16,80,32,128]{3,2,1,0:T(8,128)(2,1)}), bf16[16,80,32,128]{3,2,1,0:T(8,128)(2,1)}, u32[]{:S(2)}, u32[]{:S(2)}) %all-to-all-start.1) | async-done | bytes 10485792 | tf_op jit(solution)/shard_map/all_to_all | solution.py:320
  291.4 18.5 %outer_factors.5 = bf16[32,16,64,128]{3,2,1,0:T(8,128)(2,1)S(1)} custom-call(bf16[16,80,32,128]{3,2,1,0:T(8,128)(2,1)} %all-to-all-done.1.recv_ref, bf16[192,64,512]{2,1,0:T(8,128)(2,1)} %kernel_ref.5, bf16[512,512]{1,0:T(8,128)(2,1)S(1)} %copy-done.14, bf16[512,512]{1,0:T(8,128)(2,1)S(1)} %copy-done.15, f32[512,128]{1,0:T(8,128)S(1)} %copy.19.twiddle_ref), custom_call_target="tpu_custom_call" | custom-call | flops 8589934592 | bytes 25165824 | tf_op jit(solution)/shard_map/outer_factors/pallas_call | solution.py:185
  309.9 186.8 %all_to_all.25 = bf16[32,16,64,128]{3,2,1,0:T(8,128)(2,1)} all-to-all(bf16[32,16,64,128]{3,2,1,0:T(8,128)(2,1)S(1)} %outer_factors.5), channel_id=1, replica_groups=mesh['seq'=16,'chan'=2] {'seq','chan'}, dimensions={0} | all-to-all | bytes 16777216 | tf_op jit(solution)/shard_map/all_to_all | solution.py:320
  496.7 5.2 all-to-all-start.2
  501.9 0.0 copy-start
  501.9 4.6 copy-done
  506.5 3.0 turn_gating.3.gating_ref
  509.4 0.0 copy-start.8
  509.4 1.4 copy-done.8
  510.8 3.0 turn_gating.5.gating_ref
  513.8 1.3 copy-done.6
  515.1 11.8 %turn_gating.4.gating_ref = bf16[2,4,2,16,16,1024]{5,4,3,2,1,0:T(8,128)(2,1)S(1)} custom-call(bf16[2,192,16,1024]{3,2,1,0:T(8,128)(2,1)S(1)} %bitcast.14), custom_call_target="tpu_custom_call" | custom-call | flops 4194304 | bytes 16777216 | tf_op jit(solution)/shard_map/turn_gating/pallas_call | solution.py:210
  526.9 0.0 copy-start.3
  526.9 3.4 copy-done.3
  530.3 6.9 %outer_factors.4 = bf16[32,16,16,128]{3,2,1,0:T(8,128)(2,1)} custom-call(bf16[16,80,32,128]{3,2,1,0:T(8,128)(2,1)} %all-to-all-done.1.recv_ref, bf16[192,64,512]{2,1,0:T(8,128)(2,1)} %kernel_ref.5, bf16[512,512]{1,0:T(8,128)(2,1)S(1)} %copy-done.14, bf16[512,512]{1,0:T(8,128)(2,1)S(1)} %copy-done.15, f32[512,128]{1,0:T(8,128)S(1)} %copy.19.twiddle_ref), custom_call_target="tpu_custom_call" | custom-call | flops 2147483648 | bytes 6291456 | tf_op jit(solution)/shard_map/outer_factors/pallas_call | solution.py:185
  537.3 11.2 %all-to-all-done.2 = bf16[32,16,16,128]{3,2,1,0:T(8,128)(2,1)S(1)} async-done(((bf16[32,16,16,128]{3,2,1,0:T(8,128)(2,1)}), bf16[32,16,16,128]{3,2,1,0:T(8,128)(2,1)S(1)}, u32[]{:S(2)}, u32[]{:S(2)}) %all-to-all-start.2) | async-done | bytes 2097184 | tf_op jit(solution)/shard_map/all_to_all | solution.py:320
  548.5 1.3 copy-done.12
  549.8 5.9 all-to-all-start.4
  555.7 0.0 copy-start.16
  555.7 2.9 copy.20
  558.6 0.1 reshape.26
  558.8 0.2 copy.24.refs_3_
  559.0 0.0 copy-start.9
  559.0 1.6 copy-done.9
  560.6 1.6 copy-done.13
  562.2 2.9 last_factor.3.refs_0_
  565.1 1.3 copy-done.10
  566.4 3.4 copy-done.2
  569.7 13.3 %last_factor.4.refs_1_ = bf16[2,4,2,16,16,1024]{5,4,3,2,1,0:T(8,128)(2,1)S(1)} custom-call(bf16[16,2,16,64,128]{4,3,2,1,0:T(8,128)(2,1)S(1)} %bitcast.18, bf16[1024,1024]{1,0:T(8,128)(2,1)S(1)} %bitcast.16, bf16[2,4,2,16,16,1024]{5,4,3,2,1,0:T(8,128)(2,1)} %copy-done.3), custom_call_target="tpu_custom_call" | custom-call | flops 8589934592 | bytes 25165824 | tf_op jit(solution)/shard_map/last_factor/pallas_call | solution.py:233
  583.0 0.0 copy-start.4
  583.0 3.4 copy-done.4
  586.4 15.9 %all-to-all-done.4 = bf16[32,16,16,128]{3,2,1,0:T(8,128)(2,1)} async-done(((bf16[32,16,16,128]{3,2,1,0:T(8,128)(2,1)}), bf16[32,16,16,128]{3,2,1,0:T(8,128)(2,1)}, u32[]{:S(2)}, u32[]{:S(2)}) %all-to-all-start.4) | async-done | bytes 2097184 | tf_op jit(solution)/shard_map/all_to_all | solution.py:320
  602.3 1.6 copy-done.7
  603.9 4.1 last_factor.5.refs_2_
  608.0 0.0 copy-done.5
  608.0 0.0 copy-start.11
  608.1 1.6 copy-done.11
  609.6 13.0 %projection.1 = bf16[384,16,1024]{2,1,0:T(8,128)(2,1)} custom-call(bf16[2,1,2,16,16,1024]{5,4,3,2,1,0:T(8,128)(2,1)S(1)} %copy-done.11, bf16[2,4,2,16,16,1024]{5,4,3,2,1,0:T(8,128)(2,1)S(1)} %copy-done.5, bf16[2,1,2,16,16,1024]{5,4,3,2,1,0:T(8,128)(2,1)S(1)} %last_factor.5.refs_2_, bf16[384,384]{1,0:T(8,128)(2,1)S(1)} %copy.24.refs_3_), custom_call_target="tpu_custom_call" | custom-call | flops 4831838208 | bytes 25165824 | tf_op jit(solution)/shard_map/projection/pallas_call | solution.py:259
  (15 shorter events, 0.1 us)
Async XLA Ops:
  5.7 53.5 %all-to-all-start = ((bf16[16,16,32,128]{3,2,1,0:T(8,128)(2,1)}), bf16[16,16,32,128]{3,2,1,0:T(8,128)(2,1)S(1)}, u32[]{:S(2)}, u32[]{:S(2)}) async-start(bf16[16,16,32,128]{3,2,1,0:T(8,128)(2,1)} %first_factor.3), calls=%async_computation | async-start | bytes 4194304 | tf_op jit(solution)/shard_map/all_to_all | solution.py:320
  29.7 34.5 %copy-start.17 = (f32[64,512]{1,0:T(8,128)S(1)}, f32[64,512]{1,0:T(8,128)}, u32[]{:S(2)}) copy-start(f32[64,512]{1,0:T(8,128)} %param.17) | copy-start | bytes 393220
  29.7 36.3 %copy-start.14 = (bf16[512,512]{1,0:T(8,128)(2,1)S(1)}, bf16[512,512]{1,0:T(8,128)(2,1)}, u32[]{:S(2)}) copy-start(bf16[512,512]{1,0:T(8,128)(2,1)} %second_ref.5) | copy-start | bytes 1572868
  29.8 36.3 %copy-start.15 = (bf16[512,512]{1,0:T(8,128)(2,1)S(1)}, bf16[512,512]{1,0:T(8,128)(2,1)}, u32[]{:S(2)}) copy-start(bf16[512,512]{1,0:T(8,128)(2,1)} %back_ref.5) | copy-start | bytes 1572868
  59.2 232.2 %all-to-all-start.1 = ((bf16[16,80,32,128]{3,2,1,0:T(8,128)(2,1)}), bf16[16,80,32,128]{3,2,1,0:T(8,128)(2,1)}, u32[]{:S(2)}, u32[]{:S(2)}) async-start(bf16[16,80,32,128]{3,2,1,0:T(8,128)(2,1)} %first_factor.2), calls=%async_computation.1 | async-start | bytes 20971520 | tf_op jit(solution)/shard_map/all_to_all | solution.py:320
  66.1 4.6 copy-start.1
  496.7 51.8 %all-to-all-start.2 = ((bf16[32,16,16,128]{3,2,1,0:T(8,128)(2,1)}), bf16[32,16,16,128]{3,2,1,0:T(8,128)(2,1)S(1)}, u32[]{:S(2)}, u32[]{:S(2)}) async-start(bf16[32,16,16,128]{3,2,1,0:T(8,128)(2,1)} %outer_factors.3), calls=%async_computation.2 | async-start | bytes 4194304 | tf_op jit(solution)/shard_map/all_to_all | solution.py:320
  501.9 4.6 copy-start
  509.4 1.4 copy-start.8
  513.8 1.3 copy-start.6
  526.9 3.4 copy-start.3
  548.5 1.3 copy-start.12
  549.8 52.5 %all-to-all-start.4 = ((bf16[32,16,16,128]{3,2,1,0:T(8,128)(2,1)}), bf16[32,16,16,128]{3,2,1,0:T(8,128)(2,1)}, u32[]{:S(2)}, u32[]{:S(2)}) async-start(bf16[32,16,16,128]{3,2,1,0:T(8,128)(2,1)} %outer_factors.4), calls=%async_computation.4 | async-start | bytes 4194304 | tf_op jit(solution)/shard_map/all_to_all | solution.py:320
  555.7 2.9 copy-start.16
  559.0 1.6 copy-start.9
  560.6 1.6 copy-start.13
  565.1 1.3 copy-start.10
  566.4 3.4 copy-start.2
  583.0 3.4 copy-start.4
  602.3 1.6 copy-start.7
  603.9 4.1 copy-start.5
  608.0 1.6 copy-start.11
